TPU v7x, 512 devices: a whole 4x4x16 slice. The times are simulated.
512 devices in a mesh: tok: 16 (over z_lo, core), exp: 32 (over z_hi, x, y).
Axes of the slice: x: 4, y: 4, z: 16 (z_hi: 2, z_lo: 8; z = z_hi * 8 + z_lo), core: 2. Of those that a mesh axis runs over, the one named last changes fastest.
Arguments:
- patches: bfloat16 [4096, 1280], P('tok', 'exp'), may hold values from -30 to 30
- router: bfloat16 [128, 1280], P('exp'), may hold values from -150 to 150
- w_in: bfloat16 [32, 5120, 1280], P('exp', 'tok'), may hold values from -0.15625 to 0.15625
- w_out: bfloat16 [32, 5120, 1280], P('exp', 'tok'), may hold values from -0.078125 to 0.078125
- grad_mixed: bfloat16 [4096, 1280], P('tok', 'exp'), may hold values from -6 to 6
Outputs:
- mixed: bfloat16 [4096, 1280], P(('tok', 'exp'))
- grad_patches: bfloat16 [4096, 1280], P(('tok', 'exp'))
- grad_router: bfloat16 [128, 1280], P('exp')
- grad_w_in: bfloat16 [32, 5120, 1280], P('exp', 'tok')
- grad_w_out: bfloat16 [32, 5120, 1280], P('exp', 'tok')
All inputs are finite; a program needn't handle non-finite values.
Results may differ from a plain program's by a relative error of at most 0.035.
Values may be sent and summed in bfloat16 or wider, within the bound.
No kernel may reach another device: no remote copies, remote signals or barrier semaphores. Data moves between devices by JAX's collectives and lax.ppermute only.
A program may use at most 64 MiB of HBM per device.

v0:
```python
import math

import jax
import jax.numpy as jnp
from jax import lax
from jax.sharding import PartitionSpec as P

tanh_coef = 0.7978845608028654
cubic_coef = 0.044715


def gelu_value(inputs):
    return jax.nn.gelu(inputs, approximate=True)


def gelu_slope(inputs):
    inner = tanh_coef * (inputs + cubic_coef * inputs * inputs * inputs)
    hyper = jnp.tanh(inner)
    return 0.5 * (1.0 + hyper) + 0.5 * inputs * (1.0 - hyper * hyper) * tanh_coef * (
        1.0 + 3.0 * cubic_coef * inputs * inputs
    )


def contract_first(left, right):
    return lax.dot_general(
        left, right, (((0,), (0,)), ((), ())), preferred_element_type=jnp.float32
    )


def contract_last(left, right):
    return lax.dot_general(
        left, right, (((1,), (1,)), ((), ())), preferred_element_type=jnp.float32
    )


def body(patches, router, w_in, w_out, grad_mixed):
    gathered = lax.all_gather(patches, "exp", axis=1, tiled=True)
    score_scale = 1.0 / math.sqrt(gathered.shape[1])
    logits = contract_last(router, gathered) * score_scale
    slot_top = lax.pmax(jnp.max(logits, axis=1), "tok")
    slot_sum = lax.psum(jnp.sum(jnp.exp(logits - slot_top[:, None]), axis=1), "tok")
    patch_top = lax.pmax(jnp.max(logits, axis=0), "exp")
    patch_sum = lax.psum(jnp.sum(jnp.exp(logits - patch_top[None, :]), axis=0), "exp")
    disp_prob = jnp.exp(logits - slot_top[:, None]) / slot_sum[:, None]
    comb_prob = jnp.exp(logits - patch_top[None, :]) / patch_sum[None, :]
    dispatch = disp_prob.astype(jnp.bfloat16)
    combine = comb_prob.astype(jnp.bfloat16)
    slot_part = jnp.dot(dispatch, gathered, preferred_element_type=jnp.float32)
    slot_in = lax.psum(slot_part, "tok").astype(jnp.bfloat16)
    pre_act = contract_last(slot_in, w_in[0])
    hidden = gelu_value(pre_act).astype(jnp.bfloat16)
    out_part = jnp.dot(hidden, w_out[0], preferred_element_type=jnp.float32)
    slot_out = lax.psum(out_part, "tok").astype(jnp.bfloat16)
    mixed = lax.psum_scatter(
        contract_first(combine, slot_out), "exp", scatter_dimension=0, tiled=True
    )
    mixed = mixed.astype(jnp.bfloat16)
    cotangent = lax.all_gather(grad_mixed, "exp", axis=1, tiled=True)
    grad_comb = contract_last(slot_out, cotangent)
    grad_out_part = jnp.dot(combine, cotangent, preferred_element_type=jnp.float32)
    grad_slot_out = lax.psum(grad_out_part, "tok").astype(jnp.bfloat16)
    grad_w_out = contract_first(hidden, grad_slot_out).astype(jnp.bfloat16)[None]
    grad_hidden = contract_last(grad_slot_out, w_out[0])
    grad_pre = (grad_hidden * gelu_slope(pre_act)).astype(jnp.bfloat16)
    grad_w_in = contract_first(grad_pre, slot_in).astype(jnp.bfloat16)[None]
    grad_in_part = jnp.dot(grad_pre, w_in[0], preferred_element_type=jnp.float32)
    grad_slot_in = lax.psum(grad_in_part, "tok").astype(jnp.bfloat16)
    grad_disp = contract_last(grad_slot_in, gathered)
    patch_dot = lax.psum(jnp.sum(comb_prob * grad_comb, axis=0), "exp")
    slot_dot = lax.psum(jnp.sum(disp_prob * grad_disp, axis=1), "tok")
    grad_logits = disp_prob * (grad_disp - slot_dot[:, None]) + comb_prob * (
        grad_comb - patch_dot[None, :]
    )
    scaled = (grad_logits * score_scale).astype(jnp.bfloat16)
    router_part = jnp.dot(scaled, gathered, preferred_element_type=jnp.float32)
    grad_router = lax.psum(router_part, "tok").astype(jnp.bfloat16)
    grad_patches = lax.psum_scatter(
        contract_first(dispatch, grad_slot_in) + contract_first(scaled, router),
        "exp",
        scatter_dimension=0,
        tiled=True,
    )
    return (mixed, grad_patches.astype(jnp.bfloat16), grad_router, grad_w_in, grad_w_out)


def solution(mesh):
    return jax.shard_map(
        body,
        mesh=mesh,
        in_specs=(
            P("tok", "exp"),
            P("exp", None),
            P("exp", "tok", None),
            P("exp", "tok", None),
            P("tok", "exp"),
        ),
        out_specs=(
            P(("tok", "exp"), None),
            P(("tok", "exp"), None),
            P("exp", None),
            P("exp", "tok", None),
            P("exp", "tok", None),
        ),
        check_vma=False,
    )
```

profile of v0, /device:TPU:1, one launch (start us, length us, event | category | flops | bytes accessed | tf_op | source)
XLA Modules:
  0.0 1475.7 jit_solution(7250176129407123340)
XLA Ops:
  7.2 0.0 reduce-scatter.3.cloned.1.call-start
  7.2 154.3 %all_gather.6 = bf16[256,1280]{0,1:T(8,128)(2,1)S(1)} all-gather(bf16[256,40]{0,1:T(8,128)(2,1)} %param.5), channel_id=1, replica_groups=mesh['tok'=16,'exp'=32] {'exp'}, dimensions={1}, use_global_device_ids=true | all-gather | bytes 675840 | tf_op jit(solution)/shard_map/all_gather | solution.py:37
  161.6 1.1 fusion.52
  162.7 133.1 %pmax.14 = f32[256]{0:T(256)S(1)} all-reduce(f32[256]{0:T(256)S(1)} %get-tuple-element.9), channel_id=1, replica_groups=mesh['tok'=16,'exp'=32] {'exp'}, use_global_device_ids=true, to_apply=%region_1.0 | all-reduce | flops 256 | bytes 2048 | tf_op jit(solution)/shard_map/pmax | solution.py:42
  295.8 72.4 %pmax.15 = f32[4]{0:T(128)S(1)} all-reduce(f32[4]{0:T(128)S(1)} %get-tuple-element.10), channel_id=1, replica_groups=mesh['tok'=16,'exp'=32] {'tok'}, use_global_device_ids=true, to_apply=%region_5.0 | all-reduce | flops 4 | bytes 32 | tf_op jit(solution)/shard_map/pmax | solution.py:40
  368.2 0.2 fusion.36
  368.4 45.2 %psum.64 = f32[4]{0:T(128)S(1)} all-reduce(f32[4]{0:T(128)S(1)} %get-tuple-element.8), channel_id=1, replica_groups=mesh['tok'=16,'exp'=32] {'tok'}, use_global_device_ids=true, to_apply=%region_7.0 | all-reduce | flops 4 | bytes 32 | tf_op jit(solution)/shard_map/psum | solution.py:41
  413.6 0.3 fusion.40
  413.9 137.6 %all_gather.7 = bf16[256,1280]{0,1:T(8,128)(2,1)S(1)} all-gather(bf16[256,40]{0,1:T(8,128)(2,1)S(1)} %copy-done.3), channel_id=1, replica_groups=mesh['tok'=16,'exp'=32] {'exp'}, dimensions={1}, use_global_device_ids=true | all-gather | bytes 675840 | tf_op jit(solution)/shard_map/all_gather | solution.py:58
  551.5 132.6 %psum.63 = f32[256]{0:T(256)S(1)} all-reduce(f32[256]{0:T(256)S(1)} %get-tuple-element.7), channel_id=1, replica_groups=mesh['tok'=16,'exp'=32] {'exp'}, use_global_device_ids=true, to_apply=%region_3.0 | all-reduce | flops 256 | bytes 2048 | tf_op jit(solution)/shard_map/psum | solution.py:43
  684.2 0.3 fusion.42
  684.5 108.2 %all-reduce.1 = (bf16[4,1280]{1,0:T(4,128)(2,1)S(1)}, bf16[4,1280]{1,0:T(4,128)(2,1)S(1)}) all-reduce(f32[4,1280]{1,0:T(4,128)S(1)} %fusion.40, f32[4,1280]{1,0:T(4,128)S(1)} %fusion.42), channel_id=1, replica_groups=mesh['tok'=16,'exp'=32] {'tok'}, use_global_device_ids=true, to_apply=%region_8.0 | all-reduce | flops 10240 | bytes 61440 | tf_op jit(solution)/shard_map/psum | solution.py:49
  792.7 0.3 fusion.8
  793.0 0.3 fusion.4
  793.2 0.3 fusion.2
  793.5 0.2 fusion.6
  793.8 89.0 %all-reduce = (bf16[4,1280]{1,0:T(4,128)(2,1)S(1)}, bf16[4,1280]{1,0:T(4,128)(2,1)S(1)}) all-reduce(f32[4,1280]{1,0:T(4,128)S(1)} %fusion.4, f32[4,1280]{1,0:T(4,128)S(1)} %fusion.6), channel_id=1, replica_groups=mesh['tok'=16,'exp'=32] {'tok'}, use_global_device_ids=true, to_apply=%region_9.0 | all-reduce | flops 10240 | bytes 61440 | tf_op jit(solution)/shard_map/psum | solution.py:53
  882.8 1.5 fusion.31
  884.3 0.0 reduce-scatter.5.cloned.1.call-start
  884.3 0.2 fusion.53
  884.5 0.4 multiply_reduce_fusion.1
  884.9 53.4 %psum.69 = f32[4]{0:T(128)S(1)} all-reduce(f32[4]{0:T(128)S(1)} %get-tuple-element.5), channel_id=1, replica_groups=mesh['tok'=16,'exp'=32] {'tok'}, use_global_device_ids=true, to_apply=%region_14.0 | all-reduce | flops 4 | bytes 32 | tf_op jit(solution)/shard_map/psum | solution.py:70
  938.3 135.1 %psum.70 = f32[256]{0:T(256)S(1)} all-reduce(f32[256]{0:T(256)S(1)} %get-tuple-element.6), channel_id=1, replica_groups=mesh['tok'=16,'exp'=32] {'exp'}, use_global_device_ids=true, to_apply=%region_16.0 | all-reduce | flops 256 | bytes 2048 | tf_op jit(solution)/shard_map/psum | solution.py:69
  1073.5 0.5 fusion.25
  1073.9 1.5 convolution_add_fusion
  1075.5 0.3 fusion.51
  1075.8 95.6 %psum.71 = bf16[4,1280]{1,0:T(4,128)(2,1)} all-reduce(f32[4,1280]{1,0:T(4,128)S(1)} %fusion.51), channel_id=1, replica_groups=mesh['tok'=16,'exp'=32] {'tok'}, use_global_device_ids=true, to_apply=%region_18.0 | all-reduce | flops 5120 | bytes 30720 | tf_op jit(solution)/shard_map/psum | solution.py:76
  1171.4 1.3 fusion
  1172.7 1.3 fusion.1
  1174.0 1.4 convert_element_type.47
  1175.4 292.1 %reduce-scatter.5.cloned.1.call-done = f32[8,1280]{1,0:T(8,128)} async-done(((f32[256,1280]{1,0:T(8,128)}), f32[8,1280]{1,0:T(8,128)}) %reduce-scatter.5.cloned.1.call-update) | async-done | bytes 40976 | tf_op jit(solution)/shard_map/reduce_scatter | solution.py:77
  1467.5 1.4 convert_element_type.52
  (11 shorter events, 0.1 us)
Async XLA Ops:
  7.2 785.8 %copy-start = (bf16[1,320,1280]{2,1,0:T(8,128)(2,1)S(1)}, bf16[1,320,1280]{2,1,0:T(8,128)(2,1)}, u32[]{:S(2)}) copy-start(bf16[1,320,1280]{2,1,0:T(8,128)(2,1)} %param.8) | copy-start | bytes 2457604
  7.2 406.7 %copy-start.3 = (bf16[256,40]{0,1:T(8,128)(2,1)S(1)}, bf16[256,40]{0,1:T(8,128)(2,1)}, u32[]{:S(2)}) copy-start(bf16[256,40]{0,1:T(8,128)(2,1)} %param.9) | copy-start | bytes 61444
  7.2 1166.9 %reduce-scatter.3.cloned.1.call-start = ((), (), s32[]{:S(2)}) async-start(), calls=%async_computation.2 | async-start | bytes 1351680 | tf_op jit(solution)/shard_map/reduce_scatter | solution.py:54
  161.6 631.1 %copy-start.1 = (bf16[1,320,1280]{2,1,0:T(8,128)(2,1)S(1)}, bf16[1,320,1280]{2,1,0:T(8,128)(2,1)}, u32[]{:S(2)}) copy-start(bf16[1,320,1280]{2,1,0:T(8,128)(2,1)} %param.7) | copy-start | bytes 2457604
  884.3 189.7 %copy-start.2 = (bf16[4,1280]{1,0:T(4,128)(2,1)S(1)}, bf16[4,1280]{1,0:T(4,128)(2,1)}, u32[]{:S(2)}) copy-start(bf16[4,1280]{1,0:T(4,128)(2,1)} %param.6) | copy-start | bytes 30724
  884.3 583.2 %reduce-scatter.5.cloned.1.call-start = ((), (), s32[]{:S(2)}) async-start(), calls=%async_computation.3 | async-start | bytes 1351680 | tf_op jit(solution)/shard_map/reduce_scatter | solution.py:77
Sparse Core Ops, SparseCore 0:
  884.4 281.6 reduce-scatter.2
  1169.1 298.3 reduce-scatter.4
where the time goes:
time: 1500 us; the launch traced here: 1480 us
  blocking collectives  1160 us (77%)
  waiting for transfers between devices  292 us (19%)
    reduce_scatter x1, waiting for transfers between devices, body(): lax.psum_scatter(contract_first(dispatch, grad_slot_in) + contract_first(...  292 us
    all_gather x1, blocking collectives, body(): gathered = lax.all_gather(patches, 'exp', axis=1, tiled=True)  154 us
    all_gather x1, blocking collectives, body(): cotangent = lax.all_gather(grad_mixed, 'exp', axis=1, tiled=True)  138 us
    psum x1, blocking collectives, body(): patch_dot = lax.psum(jnp.sum(comb_prob * grad_comb, axis=0), 'exp')  135 us
    pmax x1, blocking collectives, body(): patch_top = lax.pmax(jnp.max(logits, axis=0), 'exp')  133 us
    psum x1, blocking collectives, body(): lax.psum(jnp.sum(jnp.exp(logits - patch_top[None, :]), axis=0), 'exp')  133 us
    psum x1, blocking collectives, body(): slot_in = lax.psum(slot_part, 'tok').astype(jnp.bfloat16)  108 us
    psum x1, blocking collectives, body(): grad_router = lax.psum(router_part, 'tok').astype(jnp.bfloat16)  95.6 us
  transfers between devices with their start and end apart: 2, of which 1 were waited for; matrix products, arithmetic and copies ran while one was open for 0% of the time, Pallas kernels for 0%

commit v1 on v0

v1 whole, which is shorter than its diff:
```python
import math

import jax
import jax.numpy as jnp
from jax import lax
from jax.sharding import Mesh, PartitionSpec as P

tanh_coef = 0.7978845608028654
cubic_coef = 0.044715
f32 = jnp.float32
bf16 = jnp.bfloat16
swap = [(0, 1), (1, 0)]


def gelu_value(inputs):
    return jax.nn.gelu(inputs, approximate=True)


def gelu_slope(inputs):
    inner = tanh_coef * (inputs + cubic_coef * inputs * inputs * inputs)
    hyper = jnp.tanh(inner)
    return 0.5 * (1.0 + hyper) + 0.5 * inputs * (1.0 - hyper * hyper) * tanh_coef * (
        1.0 + 3.0 * cubic_coef * inputs * inputs
    )


def contract(left, right, left_dim, right_dim):
    return lax.dot_general(
        left, right, (((left_dim,), (right_dim,)), ((), ())), preferred_element_type=f32
    )


def split(value, terms):
    out = []
    for _ in range(terms):
        head = lax.reduce_precision(value, 8, 7)
        out.append(head.astype(bf16))
        value = value - head
    return out


def spread(block, axes, count):
    return lax.all_to_all(
        jnp.broadcast_to(block[None], (count,) + block.shape), axes, 0, 0, tiled=True
    )


def body(patches, router, w_in, w_out, grad_mixed):
    core = lax.axis_index("core")
    expert = lax.axis_index(("zh", "x", "y"))
    low = core == 0
    width = router.shape[1]
    half = width // 2
    scale = 1.0 / math.sqrt(width)

    def mine(array):
        return jnp.where(low, array[:, :half], array[:, half:])

    def other(array):
        return jnp.where(low, array[:, half:], array[:, :half])

    def whole(own, got):
        return jnp.concatenate([jnp.where(low, own, got), jnp.where(low, got, own)], axis=1)

    rows = router.reshape(4, 5, 256).transpose(1, 0, 2).reshape(20, 256)
    packed = jnp.concatenate([patches.T, grad_mixed.T, rows], axis=0)
    got = spread(packed, ("zh", "x", "y"), 32)
    patches_t = got[:, :40].reshape(width, 256)
    cotangent_t = got[:, 40:80].reshape(width, 256)
    router_all = got[:, 80:].reshape(32, 5, 4, 256).transpose(0, 2, 1, 3).reshape(128, width)

    logits = contract(router_all, patches_t, 1, 0) * scale
    comb_exp = jnp.exp(logits - jnp.max(logits, axis=0, keepdims=True))
    comb_prob = comb_exp / jnp.sum(comb_exp, axis=0, keepdims=True)
    combine = comb_prob.astype(bf16)
    top = jnp.max(logits, axis=1)
    disp_exp = jnp.exp(logits - top[:, None])
    total = jnp.sum(disp_exp, axis=1)

    own_exp = lax.dynamic_slice_in_dim(disp_exp, 4 * expert, 4, 0)
    own_comb = lax.dynamic_slice_in_dim(combine, 4 * expert, 4, 0)
    slot_part = contract(jnp.concatenate(split(own_exp, 3), axis=0), patches_t, 1, 1)
    slot_part = slot_part[0:4] + slot_part[4:8] + slot_part[8:12]
    grad_part = contract(own_comb, cotangent_t, 1, 1)

    both = jnp.concatenate([slot_part, grad_part], axis=0)
    stats = jnp.concatenate([top[None], total[None], jnp.zeros((6, 128), f32)], axis=0)
    got = lax.ppermute(jnp.concatenate([other(both), stats], axis=1), "core", swap)
    top_b, total_b = got[0, half:], got[1, half:]
    top_ab = jnp.maximum(top, top_b)
    scale_a, scale_b = jnp.exp(top - top_ab), jnp.exp(top_b - top_ab)
    total = total * scale_a + total_b * scale_b

    def own(vector):
        return lax.dynamic_slice_in_dim(vector, 4 * expert, 4, vector.ndim - 1)

    both = mine(both)
    both = jnp.concatenate(
        [
            both[:4] * own(scale_a)[:, None] + got[:4, :half] * own(scale_b)[:, None],
            both[4:] + got[4:, :half],
        ],
        axis=0,
    )
    stats = jnp.concatenate([top_ab[None], total[None], jnp.zeros((6, 128), f32)], axis=0)
    got = spread(jnp.concatenate([both, stats], axis=1), "zl", 8)
    tops = got[:, 0, half:]
    slot_top = jnp.max(tops, axis=0)
    scales = jnp.exp(tops - slot_top)
    slot_sum = jnp.sum(got[:, 1, half:] * scales, axis=0)
    slot_half = jnp.sum(got[:, :4, :half] * own(scales)[:, :, None], axis=0) / own(slot_sum)[:, None]
    grad_half = jnp.sum(got[:, 4:, :half], axis=0)
    halves = jnp.concatenate([slot_half, grad_half], axis=0).astype(bf16)
    halves = whole(halves, lax.ppermute(halves, "core", swap))
    slot_in, grad_slot_out = halves[:4], halves[4:]

    pre_act = contract(slot_in, w_in[0], 1, 1)
    hidden = gelu_value(pre_act).astype(bf16)
    grad_hidden = contract(grad_slot_out, w_out[0], 1, 1)
    grad_pre = (grad_hidden * gelu_slope(pre_act)).astype(bf16)
    out_part = contract(hidden, w_out[0], 1, 0)
    grad_in_part = contract(grad_pre, w_in[0], 1, 0)
    grad_w_out = contract(hidden, grad_slot_out, 0, 0).astype(bf16)[None]
    grad_w_in = contract(grad_pre, slot_in, 0, 0).astype(bf16)[None]

    parts = jnp.concatenate([out_part, grad_in_part], axis=0)
    parts = mine(parts) + lax.ppermute(other(parts), "core", swap)
    block = jnp.concatenate([parts.astype(bf16)] + split(slot_half, 2), axis=0)
    got = spread(block, ("zh", "zl"), 16).reshape(2, 8, 16, half)
    sums = jnp.sum(got[:, :, :8].astype(f32), axis=1).astype(bf16)
    slot_pair = got[:, 0, 8:12].astype(f32) + got[:, 0, 12:].astype(f32)
    dots = jnp.sum(sums[:, 4:].astype(f32) * slot_pair, axis=2)
    dots = jnp.stack(split(dots, 3), axis=-1)
    dots = jnp.pad(dots, ((0, 0), (4, 0), (0, 125)))
    block = jnp.concatenate([sums, dots], axis=2).reshape(16, half + 128)
    got = spread(block, ("x", "y"), 16).reshape(16, 2, 2, 4, half + 128)
    got = got.transpose(2, 1, 0, 3, 4).reshape(256, half + 128)
    back = lax.ppermute(got, "core", swap)
    rows = whole(got[:, :half], back[:, :half])
    slot_out, grad_slot_in = rows[:128], rows[128:]
    slot_dot = jnp.sum(
        got[128:, half : half + 3].astype(f32) + back[128:, half : half + 3].astype(f32),
        axis=1,
    )

    disp_prob = jnp.exp(logits - slot_top[:, None]) / slot_sum[:, None]
    dispatch = disp_prob.astype(bf16)
    grad_comb = contract(slot_out, cotangent_t, 1, 0)
    grad_disp = contract(grad_slot_in, patches_t, 1, 0)
    patch_dot = jnp.sum(comb_prob * grad_comb, axis=0)
    grad_logits = disp_prob * (grad_disp - slot_dot[:, None]) + comb_prob * (
        grad_comb - patch_dot[None, :]
    )
    scaled = (grad_logits * scale).astype(bf16)

    own_scaled = lax.dynamic_slice_in_dim(scaled, 4 * expert, 4, 0)
    router_part = contract(own_scaled, patches_t, 1, 1).astype(bf16)
    got = spread(router_part.reshape(8, half), ("zl", "core"), 16)
    grad_router = jnp.sum(got.astype(f32), axis=0).astype(bf16).reshape(4, width)

    def tokens(array):
        return lax.dynamic_slice_in_dim(array, 8 * expert, 8, 1)

    mixed = contract(tokens(combine), slot_out, 0, 0).astype(bf16)
    grad_patches = contract(tokens(dispatch), grad_slot_in, 0, 0) + contract(
        tokens(scaled), router_all, 0, 0
    )
    return (mixed, grad_patches.astype(bf16), grad_router, grad_w_in, grad_w_out)


def solution(mesh):
    fine = Mesh(mesh.devices.reshape(8, 2, 2, 4, 4), ("zl", "core", "zh", "x", "y"))
    tok, exp = ("zl", "core"), ("zh", "x", "y")
    return jax.shard_map(
        body,
        mesh=fine,
        in_specs=(
            P(tok, exp),
            P(exp, None),
            P(exp, tok, None),
            P(exp, tok, None),
            P(tok, exp),
        ),
        out_specs=(
            P(tok + exp, None),
            P(tok + exp, None),
            P(exp, None),
            P(exp, tok, None),
            P(exp, tok, None),
        ),
        check_vma=False,
    )
```

time: 1500 us -> 213 us (0.14); the launches traced: 1480 us -> 212 us
  blocking collectives: 1160 us -> 72.7 us
  waiting for transfers between devices: 292 us -> 51.6 us
  starting transfers between devices: 0.08 us -> 69.9 us
    psum x7 -> x0, blocking collectives: 659 us -> none  [the longest x1 135 us: body(): patch_dot = lax.psum(jnp.sum(comb_prob * grad_comb, axis=0), 'exp')]
    reduce_scatter x2 -> x0, waiting for transfers between devices: 292 us -> none  [the longest x1 292 us: body(): lax.psum_scatter(contract_first(dispatch, grad_slot_in) + contract_first(...]
    all_gather x2 -> x0, blocking collectives: 292 us -> none  [the longest x1 154 us: body(): gathered = lax.all_gather(patches, 'exp', axis=1, tiled=True)]
    pmax x2 -> x0, blocking collectives: 205 us -> none  [the longest x1 133 us: body(): patch_top = lax.pmax(jnp.max(logits, axis=0), 'exp')]
    all_to_all x0 -> x3, blocking collectives: none -> 72.7 us  [spread(): lax.all_to_all(jnp.broadcast_to(block[None], (count,) + block.shape), axe...]
    all_to_all x0 -> x2, waiting for transfers between devices: none -> 49 us  [spread(): lax.all_to_all(jnp.broadcast_to(block[None], (count,) + block.shape), axe...]
    ppermute x0 -> x4, starting transfers between devices: none -> 41.9 us  [the longest x1 24.3 us: body(): lax.ppermute(jnp.concatenate([other(both), stats], axis=1), 'core', swap)]
    all_to_all x0 -> x2, starting transfers between devices: none -> 28 us  [spread(): lax.all_to_all(jnp.broadcast_to(block[None], (count,) + block.shape), axe...]
  transfers between devices with their start and end apart: 2 -> 6, of which waited for: 1 -> 6; matrix products, arithmetic and copies ran while one was open for 0% -> 3% of each run, Pallas kernels for 0% -> 0%
where the time goes in v1:
time: 213 us; the launch traced here: 212 us
  blocking collectives  72.7 us (34%)
  starting transfers between devices  69.9 us (33%)
  waiting for transfers between devices  51.6 us (24%)
  matrix products  8.39 us (4%)
  local copies, waits for them, and re-layouts  4.83 us (2%)
  other arithmetic  3.67 us (2%)
    all_to_all x3, blocking collectives, spread(): lax.all_to_all(jnp.broadcast_to(block[None], (count,) + block.shape), axe...  72.7 us
    all_to_all x2, waiting for transfers between devices, spread(): lax.all_to_all(jnp.broadcast_to(block[None], (count,) + block.shape), axe...  49 us
    all_to_all x2, starting transfers between devices, spread(): lax.all_to_all(jnp.broadcast_to(block[None], (count,) + block.shape), axe...  28 us
    ppermute x1, starting transfers between devices, body(): lax.ppermute(jnp.concatenate([other(both), stats], axis=1), 'core', swap)  24.3 us
    ppermute x1, starting transfers between devices, body(): back = lax.ppermute(got, 'core', swap)  9.89 us
    dot_general x15, matrix products, contract(): lax.dot_general(left, right, (((left_dim,), (right_dim,)), ((), ())), pre...  8.39 us
    ppermute x1, starting transfers between devices, body(): halves = whole(halves, lax.ppermute(halves, 'core', swap))  5.43 us
  transfers between devices with their start and end apart: 6, of which 6 were waited for; matrix products, arithmetic and copies ran while one was open for 3% of the time, Pallas kernels for 0%

profile of v1, /device:TPU:1, one launch (start us, length us, event | category | flops | bytes accessed | tf_op | source)
XLA Modules:
  0.0 212.0 jit_solution(14758319087084015801)
XLA Ops:
  0.6 0.8 reshape.99
  1.5 0.8 pad_maximum_fusion.1
  2.2 1.3 broadcast_in_dim.22
  3.5 21.1 %all-to-all-start = ((bf16[32,100,256]{2,1,0:T(8,128)(2,1)}), bf16[32,100,256]{2,1,0:T(8,128)(2,1)S(1)}, u32[]{:S(2)}, u32[]{:S(2)}) async-start(bf16[32,100,256]{2,1,0:T(8,128)(2,1)} %broadcast_in_dim.22), calls=%async_computation | async-start | bytes 3407872 | tf_op jit(solution)/shard_map/all_to_all | solution.py:43
  24.7 39.7 %all-to-all-done = bf16[32,100,256]{2,1,0:T(8,128)(2,1)S(1)} async-done(((bf16[32,100,256]{2,1,0:T(8,128)(2,1)}), bf16[32,100,256]{2,1,0:T(8,128)(2,1)S(1)}, u32[]{:S(2)}, u32[]{:S(2)}) %all-to-all-start) | async-done | bytes 1638432 | tf_op jit(solution)/shard_map/all_to_all | solution.py:43
  64.9 0.3 fusion.84
  65.5 0.3 fusion.34
  65.9 0.3 fusion.56
  66.2 24.3 %collective-permute-start = (f32[8,768]{1,0:T(8,128)S(1)}, f32[8,768]{1,0:T(8,128)S(1)}, u32[]{:S(2)}, u32[]{:S(2)}) collective-permute-start(f32[8,768]{1,0:T(8,128)S(1)} %fusion.23), channel_id=1, source_target_pairs={{0,32},{32,0},{1,33},{33,1},{2,34},{34,2},{3,35},{35,3},{4,36},{36... | collective-permute-start | bytes 73736 | tf_op jit(solution)/shard_map/ppermute | solution.py:88
  90.5 0.8 collective-permute-done
  91.7 40.6 %all_to_all.25 = f32[8,8,768]{2,1,0:T(8,128)S(1)} all-to-all(f32[8,8,768]{2,1,0:T(8,128)S(1)} %broadcast_in_dim.25), channel_id=1, replica_groups=mesh['zl'=8,'core'=2,'zh'=2,'x'=4,'y'=4] {'zl'}, dimensions={0} | all-to-all | bytes 393216 | tf_op jit(solution)/shard_map/all_to_all | solution.py:43
  132.7 5.4 %collective-permute-start.1 = (bf16[8,640]{1,0:T(8,128)(2,1)S(1)}, bf16[8,640]{1,0:T(8,128)(2,1)S(1)}, u32[]{:S(2)}, u32[]{:S(2)}) collective-permute-start(bf16[8,640]{1,0:T(8,128)(2,1)S(1)} %pad_maximum_fusion.10), channel_id=1, source_target_pairs={{0,32},{32,0},{1,33},{33,1},{2,34},{34,2},{3,35},{35,3},{4,36},{36... | collective-permute-start | bytes 30728 | tf_op jit(solution)/shard_map/ppermute | solution.py:114
  138.1 0.8 collective-permute-done.1
  139.0 0.3 fusion.13
  139.2 0.3 fusion.7
  140.1 2.3 %collective-permute-start.2 = (f32[8,640]{1,0:T(8,128)S(1)}, f32[8,640]{1,0:T(8,128)S(1)}, u32[]{:S(2)}, u32[]{:S(2)}) collective-permute-start(f32[8,640]{1,0:T(8,128)S(1)} %broadcast_select_fusion.2), channel_id=1, source_target_pairs={{0,32},{32,0},{1,33},{33,1},{2,34},{34,2},{3,35},{35,3},{4,36},{36... | collective-permute-start | bytes 61448 | tf_op jit(solution)/shard_map/ppermute | solution.py:127
  142.4 0.8 collective-permute-done.2
  143.3 20.2 %all_to_all.26 = bf16[16,16,640]{2,1,0:T(8,128)(2,1)S(1)} all-to-all(bf16[16,16,640]{2,1,0:T(8,128)(2,1)S(1)} %broadcast_in_dim.26), channel_id=1, replica_groups=mesh['zl'=8,'core'=2,'zh'=2,'x'=4,'y'=4] {'zh','zl'}, dimensions={0} | all-to-all | bytes 655360 | tf_op jit(solution)/shard_map/all_to_all | solution.py:43
  163.8 11.8 %all_to_all.27 = bf16[16,16,768]{2,1,0:T(8,128)(2,1)S(1)} all-to-all(bf16[16,16,768]{2,1,0:T(8,128)(2,1)S(1)} %broadcast_in_dim.28), channel_id=1, replica_groups=mesh['zl'=8,'core'=2,'zh'=2,'x'=4,'y'=4] {'x','y'}, dimensions={0} | all-to-all | bytes 786432 | tf_op jit(solution)/shard_map/all_to_all | solution.py:43
  176.1 9.9 %collective-permute-start.3 = (bf16[256,768]{1,0:T(8,128)(2,1)S(1)}, bf16[256,768]{1,0:T(8,128)(2,1)}, u32[]{:S(2)}, u32[]{:S(2)}) collective-permute-start(bf16[256,768]{1,0:T(8,128)(2,1)S(1)} %reshape.107), channel_id=1, source_target_pairs={{0,32},{32,0},{1,33},{33,1},{2,34},{34,2},{3,35},{35,3},{4,36},{36... | collective-permute-start | bytes 1179656 | tf_op jit(solution)/shard_map/ppermute | solution.py:138
  186.0 1.3 fusion.1
  187.4 1.0 broadcast_select_fusion
  188.5 0.3 multiply_reduce_fusion
  188.8 0.9 add_reduce_fusion
  190.0 0.3 convolution_convert_fusion.3
  190.3 0.7 broadcast_in_dim.30
  191.0 6.9 %all-to-all-start.4 = ((bf16[16,8,640]{2,1,0:T(8,128)(2,1)}), bf16[16,8,640]{2,1,0:T(8,128)(2,1)S(1)}, u32[]{:S(2)}, u32[]{:S(2)}) async-start(bf16[16,8,640]{2,1,0:T(8,128)(2,1)} %broadcast_in_dim.30), calls=%async_computation.4 | async-start | bytes 327680 | tf_op jit(solution)/shard_map/all_to_all | solution.py:43
  197.9 1.3 fusion
  199.2 0.9 convolution_convert_fusion.2
  200.4 1.7 fusion.2
  202.1 9.3 %all-to-all-done.4 = bf16[16,8,640]{2,1,0:T(8,128)(2,1)S(1)} async-done(((bf16[16,8,640]{2,1,0:T(8,128)(2,1)}), bf16[16,8,640]{2,1,0:T(8,128)(2,1)S(1)}, u32[]{:S(2)}, u32[]{:S(2)}) %all-to-all-start.4) | async-done | bytes 163872 | tf_op jit(solution)/shard_map/all_to_all | solution.py:43
  211.4 0.6 reshape.108
  (70 shorter events, 3.6 us)
Async XLA Ops:
  0.6 138.6 %copy-start = (bf16[1,320,1280]{2,1,0:T(8,128)(2,1)S(1)}, bf16[1,320,1280]{2,1,0:T(8,128)(2,1)}, u32[]{:S(2)}) copy-start(bf16[1,320,1280]{2,1,0:T(8,128)(2,1)} %param.8) | copy-start | bytes 2457604
  3.5 60.9 %all-to-all-start = ((bf16[32,100,256]{2,1,0:T(8,128)(2,1)}), bf16[32,100,256]{2,1,0:T(8,128)(2,1)S(1)}, u32[]{:S(2)}, u32[]{:S(2)}) async-start(bf16[32,100,256]{2,1,0:T(8,128)(2,1)} %broadcast_in_dim.22), calls=%async_computation | async-start | bytes 3407872 | tf_op jit(solution)/shard_map/all_to_all | solution.py:43
  64.9 26.8 %copy-start.2 = (bf16[32,40,256]{2,1,0:T(8,128)(2,1)}, bf16[32,40,256]{2,1,0:T(8,128)(2,1)S(1)}, u32[]{:S(2)}) copy-start(bf16[32,40,256]{2,1,0:T(8,128)(2,1)S(1)} %get-tuple-element.15) | copy-start | bytes 1966084
  65.2 73.8 %copy-start.1 = (bf16[1,320,1280]{2,1,0:T(8,128)(2,1)S(1)}, bf16[1,320,1280]{2,1,0:T(8,128)(2,1)}, u32[]{:S(2)}) copy-start(bf16[1,320,1280]{2,1,0:T(8,128)(2,1)} %param.7) | copy-start | bytes 2457604
  65.5 26.1 %copy-start.6 = (bf16[128,256]{1,0:T(8,128)(2,1)}, bf16[128,256]{1,0:T(8,128)(2,1)S(1)}, u32[]{:S(2)}) copy-start(bf16[128,256]{1,0:T(8,128)(2,1)S(1)} %get-tuple-element.26) | copy-start | bytes 196612
  66.2 25.1 %collective-permute-start = (f32[8,768]{1,0:T(8,128)S(1)}, f32[8,768]{1,0:T(8,128)S(1)}, u32[]{:S(2)}, u32[]{:S(2)}) collective-permute-start(f32[8,768]{1,0:T(8,128)S(1)} %fusion.23), channel_id=1, source_target_pairs={{0,32},{32,0},{1,33},{33,1},{2,34},{34,2},{3,35},{35,3},{4,36},{36... | collective-permute-start | bytes 73736 | tf_op jit(solution)/shard_map/ppermute | solution.py:88
  132.7 6.3 %collective-permute-start.1 = (bf16[8,640]{1,0:T(8,128)(2,1)S(1)}, bf16[8,640]{1,0:T(8,128)(2,1)S(1)}, u32[]{:S(2)}, u32[]{:S(2)}) collective-permute-start(bf16[8,640]{1,0:T(8,128)(2,1)S(1)} %pad_maximum_fusion.10), channel_id=1, source_target_pairs={{0,32},{32,0},{1,33},{33,1},{2,34},{34,2},{3,35},{35,3},{4,36},{36... | collective-permute-start | bytes 30728 | tf_op jit(solution)/shard_map/ppermute | solution.py:114
  140.1 3.1 %collective-permute-start.2 = (f32[8,640]{1,0:T(8,128)S(1)}, f32[8,640]{1,0:T(8,128)S(1)}, u32[]{:S(2)}, u32[]{:S(2)}) collective-permute-start(f32[8,640]{1,0:T(8,128)S(1)} %broadcast_select_fusion.2), channel_id=1, source_target_pairs={{0,32},{32,0},{1,33},{33,1},{2,34},{34,2},{3,35},{35,3},{4,36},{36... | collective-permute-start | bytes 61448 | tf_op jit(solution)/shard_map/ppermute | solution.py:127
  175.7 12.7 %copy-start.3 = (bf16[32,40,256]{2,1,0:T(8,128)(2,1)S(1)}, bf16[32,40,256]{2,1,0:T(8,128)(2,1)}, u32[]{:S(2)}) copy-start(bf16[32,40,256]{2,1,0:T(8,128)(2,1)} %copy-done.2) | copy-start | bytes 1966084
  176.1 11.4 %collective-permute-start.3 = (bf16[256,768]{1,0:T(8,128)(2,1)S(1)}, bf16[256,768]{1,0:T(8,128)(2,1)}, u32[]{:S(2)}, u32[]{:S(2)}) collective-permute-start(bf16[256,768]{1,0:T(8,128)(2,1)S(1)} %reshape.107), channel_id=1, source_target_pairs={{0,32},{32,0},{1,33},{33,1},{2,34},{34,2},{3,35},{35,3},{4,36},{36... | collective-permute-start | bytes 1179656 | tf_op jit(solution)/shard_map/ppermute | solution.py:138
  188.5 1.2 copy-start.4
  188.8 1.2 copy-start.8
  189.7 9.5 %copy-start.7 = (bf16[128,256]{1,0:T(8,128)(2,1)S(1)}, bf16[128,256]{1,0:T(8,128)(2,1)}, u32[]{:S(2)}) copy-start(bf16[128,256]{1,0:T(8,128)(2,1)} %copy-done.6) | copy-start | bytes 196612
  190.0 9.2 %copy-start.5 = (bf16[256,640]{1,0:T(8,128)(2,1)S(1)}, bf16[256,640]{1,0:T(8,128)(2,1)}, u32[]{:S(2)}) copy-start(bf16[256,640]{1,0:T(8,128)(2,1)} %copy-done.4) | copy-start | bytes 983044
  191.0 20.4 %all-to-all-start.4 = ((bf16[16,8,640]{2,1,0:T(8,128)(2,1)}), bf16[16,8,640]{2,1,0:T(8,128)(2,1)S(1)}, u32[]{:S(2)}, u32[]{:S(2)}) async-start(bf16[16,8,640]{2,1,0:T(8,128)(2,1)} %broadcast_in_dim.30), calls=%async_computation.4 | async-start | bytes 327680 | tf_op jit(solution)/shard_map/all_to_all | solution.py:43

commit v2 on v1

--- a/solution.py
+++ b/solution.py
@@ -64,10 +64,15 @@
 
     rows = router.reshape(4, 5, 256).transpose(1, 0, 2).reshape(20, 256)
     packed = jnp.concatenate([patches.T, grad_mixed.T, rows], axis=0)
-    got = spread(packed, ("zh", "x", "y"), 32)
-    patches_t = got[:, :40].reshape(width, 256)
-    cotangent_t = got[:, 40:80].reshape(width, 256)
-    router_all = got[:, 80:].reshape(32, 5, 4, 256).transpose(0, 2, 1, 3).reshape(128, width)
+    partner = lax.ppermute(packed, "zh", swap)
+    first = lax.axis_index("zh") == 0
+    pair = jnp.stack([jnp.where(first, packed, partner), jnp.where(first, partner, packed)])
+    got = spread(pair, ("x", "y"), 16)
+    patches_t = got[:, :, :40].transpose(1, 0, 2, 3).reshape(width, 256)
+    cotangent_t = got[:, :, 40:80].transpose(1, 0, 2, 3).reshape(width, 256)
+    router_all = (
+        got[:, :, 80:].reshape(16, 2, 5, 4, 256).transpose(1, 0, 3, 2, 4).reshape(128, width)
+    )
 
     logits = contract(router_all, patches_t, 1, 0) * scale
     comb_exp = jnp.exp(logits - jnp.max(logits, axis=0, keepdims=True))
@@ -125,10 +130,15 @@
 
     parts = jnp.concatenate([out_part, grad_in_part], axis=0)
     parts = mine(parts) + lax.ppermute(other(parts), "core", swap)
-    block = jnp.concatenate([parts.astype(bf16)] + split(slot_half, 2), axis=0)
-    got = spread(block, ("zh", "zl"), 16).reshape(2, 8, 16, half)
-    sums = jnp.sum(got[:, :, :8].astype(f32), axis=1).astype(bf16)
-    slot_pair = got[:, 0, 8:12].astype(f32) + got[:, 0, 12:].astype(f32)
+    piece = lax.dynamic_slice_in_dim(
+        jnp.concatenate(split(slot_half, 2), axis=0), lax.axis_index("zl"), 1, 0
+    )
+    piece = jnp.pad(piece.reshape(5, 128), ((0, 3), (0, 0)))
+    block = jnp.concatenate([parts.astype(bf16), piece], axis=1)
+    got = spread(block, ("zh", "zl"), 16).reshape(2, 8, 8, half + 128)
+    sums = jnp.sum(got[..., :half].astype(f32), axis=1).astype(bf16)
+    pieces = got[:, :, :5, half:].reshape(2, 2, 4, half).astype(f32)
+    slot_pair = pieces[:, 0] + pieces[:, 1]
     dots = jnp.sum(sums[:, 4:].astype(f32) * slot_pair, axis=2)
     dots = jnp.stack(split(dots, 3), axis=-1)
     dots = jnp.pad(dots, ((0, 0), (4, 0), (0, 125)))

time: 213 us -> 160 us (0.75)
  blocking collectives: 72.7 us -> 52.4 us
  starting transfers between devices: 69.9 us -> 50.8 us
  waiting for transfers between devices: 51.6 us -> 34.1 us
  local copies, waits for them, and re-layouts: 4.83 us -> 8.04 us
    all_to_all x3, blocking collectives: 72.7 us -> 52.4 us  [spread(): lax.all_to_all(jnp.broadcast_to(block[None], (count,) + block.shape), axe...]
    all_to_all x2, waiting for transfers between devices: 49 us -> 29.9 us  [spread(): lax.all_to_all(jnp.broadcast_to(block[None], (count,) + block.shape), axe...]
    ppermute x1, starting transfers between devices: 24.3 us -> 6.35 us  [body(): lax.ppermute(jnp.concatenate([other(both), stats], axis=1), 'core', swap)]
    ppermute x0 -> x1, starting transfers between devices: none -> 16.3 us  [body(): partner = lax.ppermute(packed, 'zh', swap)]
    all_to_all x2, starting transfers between devices: 28 us -> 13.8 us  [spread(): lax.all_to_all(jnp.broadcast_to(block[None], (count,) + block.shape), axe...]
    ppermute x1, starting transfers between devices: 9.89 us -> 6.69 us  [body(): back = lax.ppermute(got, 'core', swap)]
  transfers between devices with their start and end apart: 6 -> 7, of which waited for: 6 -> 7; matrix products, arithmetic and copies ran while one was open for 3% -> 4% of each run, Pallas kernels for 0% -> 0%
where the time goes in v2:
time: 160 us; the launch traced here: 159 us
  blocking collectives  52.4 us (33%)
  starting transfers between devices  50.8 us (32%)
  waiting for transfers between devices  34.1 us (21%)
  matrix products  8.34 us (5%)
  local copies, waits for them, and re-layouts  8.04 us (5%)
  other arithmetic  4.48 us (3%)
    all_to_all x3, blocking collectives, spread(): lax.all_to_all(jnp.broadcast_to(block[None], (count,) + block.shape), axe...  52.4 us
    all_to_all x2, waiting for transfers between devices, spread(): lax.all_to_all(jnp.broadcast_to(block[None], (count,) + block.shape), axe...  29.9 us
    ppermute x1, starting transfers between devices, body(): partner = lax.ppermute(packed, 'zh', swap)  16.3 us
    all_to_all x2, starting transfers between devices, spread(): lax.all_to_all(jnp.broadcast_to(block[None], (count,) + block.shape), axe...  13.8 us
    dot_general x15, matrix products, contract(): lax.dot_general(left, right, (((left_dim,), (right_dim,)), ((), ())), pre...  8.34 us
    ppermute x1, starting transfers between devices, body(): back = lax.ppermute(got, 'core', swap)  6.69 us
    ppermute x1, starting transfers between devices, body(): lax.ppermute(jnp.concatenate([other(both), stats], axis=1), 'core', swap)  6.35 us
    ppermute x1, starting transfers between devices, body(): halves = whole(halves, lax.ppermute(halves, 'core', swap))  5.43 us
  transfers between devices with their start and end apart: 7, of which 7 were waited for; matrix products, arithmetic and copies ran while one was open for 4% of the time, Pallas kernels for 0%

profile of v2, /device:TPU:1, one launch (start us, length us, event | category | flops | bytes accessed | tf_op | source)
XLA Modules:
  0.0 159.3 jit_solution(1596176538562851490)
XLA Ops:
  0.6 0.8 reshape.103
  1.5 0.8 pad_maximum_fusion.2
  2.2 16.3 %collective-permute-start = (bf16[100,256]{1,0:T(8,128)(2,1)S(1)}, bf16[100,256]{1,0:T(8,128)(2,1)S(1)}, u32[]{:S(2)}, u32[]{:S(2)}) collective-permute-start(bf16[100,256]{1,0:T(8,128)(2,1)S(1)} %pad_maximum_fusion.2), channel_id=1, source_target_pairs={{0,16},{16,0},{1,17},{17,1},{2,18},{18,2},{3,19},{19,3},{4,20},{20... | collective-permute-start | bytes 153608 | tf_op jit(solution)/shard_map/ppermute | solution.py:67
  18.5 1.7 %collective-permute-done = bf16[100,256]{1,0:T(8,128)(2,1)S(1)} collective-permute-done((bf16[100,256]{1,0:T(8,128)(2,1)S(1)}, bf16[100,256]{1,0:T(8,128)(2,1)S(1)}, u32[]{:S(2)}, u32[]{:S(2)}) %collective-permute-start) | collective-permute-done | bytes 51232 | tf_op jit(solution)/shard_map/ppermute | solution.py:67
  20.2 0.8 select_bitcast_fusion.1
  21.1 2.0 %broadcast_in_dim.22 = bf16[16,2,100,256]{3,1,2,0:T(2,128)(2,1)} broadcast(bf16[2,100,256]{2,0,1:T(2,128)(2,1)S(1)} %copy.73), dimensions={1,2,3} | broadcast | bytes 1740800 | tf_op jit(solution)/shard_map/broadcast_in_dim | solution.py:44
  23.1 6.8 %all-to-all-start = ((bf16[16,2,100,256]{3,1,2,0:T(2,128)(2,1)}), bf16[16,2,100,256]{3,1,2,0:T(2,128)(2,1)S(1)}, u32[]{:S(2)}, u32[]{:S(2)}) async-start(bf16[16,2,100,256]{3,1,2,0:T(2,128)(2,1)} %broadcast_in_dim.22), calls=%async_computation | async-start | bytes 3276800 | tf_op jit(solution)/shard_map/all_to_all | solution.py:43
  29.9 20.6 %all-to-all-done = bf16[16,2,100,256]{3,1,2,0:T(2,128)(2,1)S(1)} async-done(((bf16[16,2,100,256]{3,1,2,0:T(2,128)(2,1)}), bf16[16,2,100,256]{3,1,2,0:T(2,128)(2,1)S(1)}, u32[]{:S(2)}, u32[]{:S(2)}) %all-to-all-start) | async-done | bytes 1638432 | tf_op jit(solution)/shard_map/all_to_all | solution.py:43
  50.5 0.9 fusion.84
  52.8 0.4 copy-done.15
  53.9 6.4 %collective-permute-start.1 = (f32[8,768]{1,0:T(8,128)S(1)}, f32[8,768]{1,0:T(8,128)S(1)}, u32[]{:S(2)}, u32[]{:S(2)}) collective-permute-start(f32[8,768]{1,0:T(8,128)S(1)} %fusion.23), channel_id=1, source_target_pairs={{0,32},{32,0},{1,33},{33,1},{2,34},{34,2},{3,35},{35,3},{4,36},{36... | collective-permute-start | bytes 73736 | tf_op jit(solution)/shard_map/ppermute | solution.py:93
  60.3 0.8 collective-permute-done.1
  61.4 22.3 %all_to_all.25 = f32[8,8,768]{2,1,0:T(8,128)S(1)} all-to-all(f32[8,8,768]{2,1,0:T(8,128)S(1)} %broadcast_in_dim.25), channel_id=1, replica_groups=mesh['zl'=8,'core'=2,'zh'=2,'x'=4,'y'=4] {'zl'}, dimensions={0} | all-to-all | bytes 393216 | tf_op jit(solution)/shard_map/all_to_all | solution.py:43
  83.8 0.4 copy-done.17
  84.6 5.4 %collective-permute-start.2 = (bf16[8,640]{1,0:T(8,128)(2,1)S(1)}, bf16[8,640]{1,0:T(8,128)(2,1)S(1)}, u32[]{:S(2)}, u32[]{:S(2)}) collective-permute-start(bf16[8,640]{1,0:T(8,128)(2,1)S(1)} %pad_maximum_fusion.10), channel_id=1, source_target_pairs={{0,32},{32,0},{1,33},{33,1},{2,34},{34,2},{3,35},{35,3},{4,36},{36... | collective-permute-start | bytes 30728 | tf_op jit(solution)/shard_map/ppermute | solution.py:119
  90.0 0.8 collective-permute-done.2
  91.1 0.3 fusion.7
  92.2 2.3 %collective-permute-start.3 = (f32[8,640]{1,0:T(8,128)S(1)}, f32[8,640]{1,0:T(8,128)S(1)}, u32[]{:S(2)}, u32[]{:S(2)}) collective-permute-start(f32[8,640]{1,0:T(8,128)S(1)} %broadcast_select_fusion.2), channel_id=1, source_target_pairs={{0,32},{32,0},{1,33},{33,1},{2,34},{34,2},{3,35},{35,3},{4,36},{36... | collective-permute-start | bytes 61448 | tf_op jit(solution)/shard_map/ppermute | solution.py:132
  94.6 0.8 collective-permute-done.3
  95.4 18.9 %all_to_all.26 = bf16[16,8,768]{2,1,0:T(8,128)(2,1)S(1)} all-to-all(bf16[16,8,768]{2,1,0:T(8,128)(2,1)S(1)} %broadcast_in_dim.26), channel_id=1, replica_groups=mesh['zl'=8,'core'=2,'zh'=2,'x'=4,'y'=4] {'zh','zl'}, dimensions={0} | all-to-all | bytes 393216 | tf_op jit(solution)/shard_map/all_to_all | solution.py:43
  114.7 11.2 %all_to_all.27 = bf16[16,16,768]{2,1,0:T(8,128)(2,1)S(1)} all-to-all(bf16[16,16,768]{2,1,0:T(8,128)(2,1)S(1)} %broadcast_in_dim.28), channel_id=1, replica_groups=mesh['zl'=8,'core'=2,'zh'=2,'x'=4,'y'=4] {'x','y'}, dimensions={0} | all-to-all | bytes 786432 | tf_op jit(solution)/shard_map/all_to_all | solution.py:43
  126.3 6.7 %collective-permute-start.4 = (bf16[256,768]{1,0:T(8,128)(2,1)S(1)}, bf16[256,768]{1,0:T(8,128)(2,1)}, u32[]{:S(2)}, u32[]{:S(2)}) collective-permute-start(bf16[256,768]{1,0:T(8,128)(2,1)S(1)} %reshape.112), channel_id=1, source_target_pairs={{0,32},{32,0},{1,33},{33,1},{2,34},{34,2},{3,35},{35,3},{4,36},{36... | collective-permute-start | bytes 1179656 | tf_op jit(solution)/shard_map/ppermute | solution.py:148
  133.1 1.3 fusion.1
  134.5 1.0 broadcast_select_fusion
  135.9 0.9 add_reduce_fusion
  137.4 0.7 broadcast_in_dim.30
  138.1 7.1 %all-to-all-start.4 = ((bf16[16,8,640]{2,1,0:T(8,128)(2,1)}), bf16[16,8,640]{2,1,0:T(8,128)(2,1)S(1)}, u32[]{:S(2)}, u32[]{:S(2)}) async-start(bf16[16,8,640]{2,1,0:T(8,128)(2,1)} %broadcast_in_dim.30), calls=%async_computation.4 | async-start | bytes 327680 | tf_op jit(solution)/shard_map/all_to_all | solution.py:43
  145.2 1.3 fusion
  146.5 0.9 convolution_convert_fusion.2
  147.7 1.7 %fusion.2 = bf16[8,1280]{1,0:T(8,128)(2,1)} fusion(f32[8,1280]{1,0:T(8,128)S(1)} %fusion.20, bf16[256,640]{1,0:T(8,128)(2,1)S(1)} %get-tuple-element.17, bf16[256,640]{1,0:T(8,128)(2,1)S(1)} %copy-done.5, f32[128,256]{1,0:T(8,128)} %copy-done.14, s32[]{:T(128)S(6)} %select_n.74), kind=kOutput, calls=%fused_computation.5 | convolution fusion | flops 3297280 | bytes 749572 | tf_op jit(solution)/shard_map/dot_general | solution.py:28
  149.4 9.3 %all-to-all-done.4 = bf16[16,8,640]{2,1,0:T(8,128)(2,1)S(1)} async-done(((bf16[16,8,640]{2,1,0:T(8,128)(2,1)}), bf16[16,8,640]{2,1,0:T(8,128)(2,1)S(1)}, u32[]{:S(2)}, u32[]{:S(2)}) %all-to-all-start.4) | async-done | bytes 163872 | tf_op jit(solution)/shard_map/all_to_all | solution.py:43
  158.7 0.6 reshape.113
  (104 shorter events, 6.1 us)
Async XLA Ops:
  0.6 90.5 %copy-start = (bf16[1,320,1280]{2,1,0:T(8,128)(2,1)S(1)}, bf16[1,320,1280]{2,1,0:T(8,128)(2,1)}, u32[]{:S(2)}) copy-start(bf16[1,320,1280]{2,1,0:T(8,128)(2,1)} %param.8) | copy-start | bytes 2457604
  2.2 18.0 %collective-permute-start = (bf16[100,256]{1,0:T(8,128)(2,1)S(1)}, bf16[100,256]{1,0:T(8,128)(2,1)S(1)}, u32[]{:S(2)}, u32[]{:S(2)}) collective-permute-start(bf16[100,256]{1,0:T(8,128)(2,1)S(1)} %pad_maximum_fusion.2), channel_id=1, source_target_pairs={{0,16},{16,0},{1,17},{17,1},{2,18},{18,2},{3,19},{19,3},{4,20},{20... | collective-permute-start | bytes 153608 | tf_op jit(solution)/shard_map/ppermute | solution.py:67
  23.1 27.4 %all-to-all-start = ((bf16[16,2,100,256]{3,1,2,0:T(2,128)(2,1)}), bf16[16,2,100,256]{3,1,2,0:T(2,128)(2,1)S(1)}, u32[]{:S(2)}, u32[]{:S(2)}) async-start(bf16[16,2,100,256]{3,1,2,0:T(2,128)(2,1)} %broadcast_in_dim.22), calls=%async_computation | async-start | bytes 3276800 | tf_op jit(solution)/shard_map/all_to_all | solution.py:43
  51.5 2.0 %copy-start.2 = (bf16[16,2,40,256]{3,2,0,1:T(8,128)(2,1)}, bf16[16,2,40,256]{3,2,0,1:T(8,128)(2,1)S(1)}, u32[]{:S(2)}) copy-start(bf16[16,2,40,256]{3,2,0,1:T(8,128)(2,1)S(1)} %copy.88) | copy-start | bytes 1966084
  52.5 8.9 %copy-start.12 = (f32[256]{0:T(256)}, f32[256]{0:T(256)S(1)}, u32[]{:S(2)}) copy-start(f32[256]{0:T(256)S(1)} %get-tuple-element.44) | copy-start | bytes 3076
  52.5 38.3 %copy-start.1 = (bf16[1,320,1280]{2,1,0:T(8,128)(2,1)S(1)}, bf16[1,320,1280]{2,1,0:T(8,128)(2,1)}, u32[]{:S(2)}) copy-start(bf16[1,320,1280]{2,1,0:T(8,128)(2,1)} %param.7) | copy-start | bytes 2457604
  52.6 0.6 copy-start.15
  53.2 8.2 %copy-start.10 = (bf16[128,256]{1,0:T(8,128)(2,1)}, bf16[128,256]{1,0:T(8,128)(2,1)S(1)}, u32[]{:S(2)}) copy-start(bf16[128,256]{1,0:T(8,128)(2,1)S(1)} %get-tuple-element.26) | copy-start | bytes 196612
  53.9 7.2 %collective-permute-start.1 = (f32[8,768]{1,0:T(8,128)S(1)}, f32[8,768]{1,0:T(8,128)S(1)}, u32[]{:S(2)}, u32[]{:S(2)}) collective-permute-start(f32[8,768]{1,0:T(8,128)S(1)} %fusion.23), channel_id=1, source_target_pairs={{0,32},{32,0},{1,33},{33,1},{2,34},{34,2},{3,35},{35,3},{4,36},{36... | collective-permute-start | bytes 73736 | tf_op jit(solution)/shard_map/ppermute | solution.py:93
  83.7 0.5 copy-start.17
  83.7 0.6 copy-start.19
  84.6 6.3 %collective-permute-start.2 = (bf16[8,640]{1,0:T(8,128)(2,1)S(1)}, bf16[8,640]{1,0:T(8,128)(2,1)S(1)}, u32[]{:S(2)}, u32[]{:S(2)}) collective-permute-start(bf16[8,640]{1,0:T(8,128)(2,1)S(1)} %pad_maximum_fusion.10), channel_id=1, source_target_pairs={{0,32},{32,0},{1,33},{33,1},{2,34},{34,2},{3,35},{35,3},{4,36},{36... | collective-permute-start | bytes 30728 | tf_op jit(solution)/shard_map/ppermute | solution.py:119
  90.8 1.4 copy-start.6
  91.1 0.6 copy-start.8
  92.2 3.1 %collective-permute-start.3 = (f32[8,640]{1,0:T(8,128)S(1)}, f32[8,640]{1,0:T(8,128)S(1)}, u32[]{:S(2)}, u32[]{:S(2)}) collective-permute-start(f32[8,640]{1,0:T(8,128)S(1)} %broadcast_select_fusion.2), channel_id=1, source_target_pairs={{0,32},{32,0},{1,33},{33,1},{2,34},{34,2},{3,35},{35,3},{4,36},{36... | collective-permute-start | bytes 61448 | tf_op jit(solution)/shard_map/ppermute | solution.py:132
  114.6 18.4 %copy-start.7 = (bf16[8,640]{1,0:T(8,128)(2,1)S(1)}, bf16[8,640]{1,0:T(8,128)(2,1)}, u32[]{:S(2)}) copy-start(bf16[8,640]{1,0:T(8,128)(2,1)} %copy-done.6) | copy-start | bytes 30724
  114.6 18.4 %copy-start.9 = (f32[4,320]{1,0:T(4,128)S(1)}, f32[4,320]{1,0:T(4,128)}, u32[]{:S(2)}) copy-start(f32[4,320]{1,0:T(4,128)} %copy-done.8) | copy-start | bytes 15364
  126.2 9.4 %copy-start.3 = (bf16[16,2,40,256]{3,2,0,1:T(8,128)(2,1)S(1)}, bf16[16,2,40,256]{3,2,0,1:T(8,128)(2,1)}, u32[]{:S(2)}) copy-start(bf16[16,2,40,256]{3,2,0,1:T(8,128)(2,1)} %copy-done.2) | copy-start | bytes 1966084
  126.2 9.4 %copy-start.13 = (f32[256]{0:T(256)S(1)}, f32[256]{0:T(256)}, u32[]{:S(2)}) copy-start(f32[256]{0:T(256)} %copy-done.12) | copy-start | bytes 3076
  126.2 9.4 %copy-start.16 = (f32[256]{0:T(256)S(1)}, f32[256]{0:T(256)}, u32[]{:S(2)}) copy-start(f32[256]{0:T(256)} %copy-done.15) | copy-start | bytes 3076
  126.2 9.4 %copy-start.18 = (f32[128]{0:T(128)S(1)}, f32[128]{0:T(128)}, u32[]{:S(2)}) copy-start(f32[128]{0:T(128)} %copy-done.17) | copy-start | bytes 1540
  126.2 9.4 %copy-start.20 = (f32[128]{0:T(128)S(1)}, f32[128]{0:T(128)}, u32[]{:S(2)}) copy-start(f32[128]{0:T(128)} %copy-done.19) | copy-start | bytes 1540
  126.3 8.2 %collective-permute-start.4 = (bf16[256,768]{1,0:T(8,128)(2,1)S(1)}, bf16[256,768]{1,0:T(8,128)(2,1)}, u32[]{:S(2)}, u32[]{:S(2)}) collective-permute-start(bf16[256,768]{1,0:T(8,128)(2,1)S(1)} %reshape.112), channel_id=1, source_target_pairs={{0,32},{32,0},{1,33},{33,1},{2,34},{34,2},{3,35},{35,3},{4,36},{36... | collective-permute-start | bytes 1179656 | tf_op jit(solution)/shard_map/ppermute | solution.py:148
  135.5 1.3 copy-start.4
  135.9 1.2 copy-start.14
  136.8 9.7 %copy-start.11 = (bf16[128,256]{1,0:T(8,128)(2,1)S(1)}, bf16[128,256]{1,0:T(8,128)(2,1)}, u32[]{:S(2)}) copy-start(bf16[128,256]{1,0:T(8,128)(2,1)} %copy-done.10) | copy-start | bytes 196612
  137.1 9.4 %copy-start.5 = (bf16[256,640]{1,0:T(8,128)(2,1)S(1)}, bf16[256,640]{1,0:T(8,128)(2,1)}, u32[]{:S(2)}) copy-start(bf16[256,640]{1,0:T(8,128)(2,1)} %copy-done.4) | copy-start | bytes 983044
  138.1 20.6 %all-to-all-start.4 = ((bf16[16,8,640]{2,1,0:T(8,128)(2,1)}), bf16[16,8,640]{2,1,0:T(8,128)(2,1)S(1)}, u32[]{:S(2)}, u32[]{:S(2)}) async-start(bf16[16,8,640]{2,1,0:T(8,128)(2,1)} %broadcast_in_dim.30), calls=%async_computation.4 | async-start | bytes 327680 | tf_op jit(solution)/shard_map/all_to_all | solution.py:43

commit v3 on v2

v3 whole, which is shorter than its diff:
```python
import math

import jax
import jax.numpy as jnp
from jax import lax
from jax.experimental import pallas as pl
from jax.experimental.pallas import tpu as pltpu
from jax.sharding import Mesh, PartitionSpec as P

tanh_coef = 0.7978845608028654
cubic_coef = 0.044715
f32 = jnp.float32
bf16 = jnp.bfloat16
swap = [(0, 1), (1, 0)]


def gelu_value(inputs):
    return jax.nn.gelu(inputs, approximate=True)


def gelu_slope(inputs):
    inner = tanh_coef * (inputs + cubic_coef * inputs * inputs * inputs)
    hyper = jnp.tanh(inner)
    return 0.5 * (1.0 + hyper) + 0.5 * inputs * (1.0 - hyper * hyper) * tanh_coef * (
        1.0 + 3.0 * cubic_coef * inputs * inputs
    )


def contract(left, right, left_dim, right_dim):
    return lax.dot_general(
        left, right, (((left_dim,), (right_dim,)), ((), ())), preferred_element_type=f32
    )


def split(value, terms):
    out = []
    for _ in range(terms):
        head = lax.reduce_precision(value, 8, 7)
        out.append(head.astype(bf16))
        value = value - head
    return out


def spread(block, axes, count):
    return lax.all_to_all(
        jnp.broadcast_to(block[None], (count,) + block.shape), axes, 0, 0, tiled=True
    )


def fan_kernel(block_ref, out_ref):
    for peer in range(out_ref.shape[0]):
        out_ref[peer] = block_ref[...]


def fan(block, count, flops):
    return pl.pallas_call(
        fan_kernel,
        out_shape=jax.ShapeDtypeStruct((count,) + block.shape, block.dtype),
        in_specs=[pl.BlockSpec(memory_space=pltpu.VMEM)],
        out_specs=pl.BlockSpec(memory_space=pltpu.VMEM),
        compiler_params=pltpu.CompilerParams(vmem_limit_bytes=16 << 20),
        cost_estimate=pl.CostEstimate(flops=flops, bytes_accessed=0, transcendentals=0),
    )(block)


def body(patches, router, w_in, w_out, grad_mixed):
    core = lax.axis_index("core")
    expert = lax.axis_index(("zh", "x", "y"))
    low = core == 0
    width = router.shape[1]
    half = width // 2
    scale = 1.0 / math.sqrt(width)

    def mine(array):
        return jnp.where(low, array[:, :half], array[:, half:])

    def other(array):
        return jnp.where(low, array[:, half:], array[:, :half])

    def whole(own, got):
        return jnp.concatenate([jnp.where(low, own, got), jnp.where(low, got, own)], axis=1)

    packed = jnp.concatenate(
        [patches.T, grad_mixed.T] + [router[:, k * 256 : k * 256 + 256] for k in range(5)], axis=0
    )
    first = lax.axis_index("zh") == 0
    far = lax.all_to_all(fan(lax.ppermute(packed, "zh", swap), 16, 10**11), ("x", "y"), 0, 0, tiled=True)
    near = spread(packed, ("x", "y"), 16)

    def ordered(start, stop):
        own, partner = near[:, start:stop], far[:, start:stop]
        return jnp.stack([jnp.where(first, own, partner), jnp.where(first, partner, own)])

    patches_t = ordered(0, 40).reshape(width, 256)
    cotangent_t = ordered(40, 80).reshape(width, 256)
    router_all = (
        ordered(80, 100).reshape(32, 5, 4, 256).transpose(0, 2, 1, 3).reshape(128, width)
    )

    logits = contract(router_all, patches_t, 1, 0) * scale
    comb_exp = jnp.exp(logits - jnp.max(logits, axis=0, keepdims=True))
    comb_prob = comb_exp / jnp.sum(comb_exp, axis=0, keepdims=True)
    combine = comb_prob.astype(bf16)
    top = jnp.max(logits, axis=1)
    total = jnp.sum(jnp.exp(logits - top[:, None]), axis=1)

    stats = jnp.stack(split(top, 3) + split(total, 3))
    got = spread(jnp.pad(stats, ((0, 2), (0, 0))), ("zl", "core"), 16).astype(f32)
    tops = got[:, 0] + got[:, 1] + got[:, 2]
    slot_top = jnp.max(tops, axis=0)
    slot_sum = jnp.sum((got[:, 3] + got[:, 4] + got[:, 5]) * jnp.exp(tops - slot_top), axis=0)
    disp_prob = jnp.exp(logits - slot_top[:, None]) / slot_sum[:, None]
    dispatch, rest = split(disp_prob, 2)

    def own(array):
        return lax.dynamic_slice_in_dim(array, 4 * expert, 4, 0)

    parts = jnp.concatenate(
        [
            contract(jnp.concatenate([own(dispatch), own(rest)], axis=0), patches_t, 1, 1),
            contract(own(combine), cotangent_t, 1, 1),
        ],
        axis=0,
    )
    parts = mine(parts) + lax.ppermute(other(parts), "core", swap)
    block = jnp.concatenate(
        split(parts[:4], 2) + [parts[4:8].astype(bf16)] + split(parts[8:], 2), axis=0
    )
    got = jnp.sum(spread(block, "zl", 8).astype(f32), axis=0)
    slot_half = got[:4] + got[4:8]
    grad_half = got[12:16] + got[16:]
    halves = jnp.concatenate([slot_half, grad_half], axis=0).astype(bf16)

    rows = w_in.shape[1]
    pair_in = jnp.concatenate([mine(w_in[0]), lax.ppermute(other(w_in[0]), "core", swap)], axis=0)
    pair_out = jnp.concatenate(
        [mine(w_out[0]), lax.ppermute(other(w_out[0]), "core", swap)], axis=0
    )
    pre = jnp.concatenate(
        [contract(halves[:4], pair_in, 1, 1), contract(halves[4:], pair_out, 1, 1)], axis=0
    )
    pre = pre + lax.ppermute(
        jnp.concatenate([pre[:, rows:], pre[:, :rows]], axis=1), "core", swap
    )
    pre_act, grad_hidden = pre[:4], pre[4:]
    hidden = gelu_value(pre_act).astype(bf16)
    grad_pre = (grad_hidden * gelu_slope(pre_act)).astype(bf16)
    parts = jnp.concatenate(
        [contract(hidden, pair_out, 1, 0), contract(grad_pre, pair_in, 1, 0)], axis=0
    )
    full = whole(halves, lax.ppermute(halves, "core", swap))
    grad_w_out = contract(hidden[:, :rows], full[4:], 0, 0).astype(bf16)[None]
    grad_w_in = contract(grad_pre[:, :rows], full[:4], 0, 0).astype(bf16)[None]

    piece = lax.dynamic_slice_in_dim(
        jnp.concatenate(split(slot_half + got[8:12], 2), axis=0), lax.axis_index("zl"), 1, 0
    )
    piece = jnp.pad(piece.reshape(5, 128), ((0, 3), (0, 0)))
    block = jnp.concatenate(split(parts, 2) + [piece], axis=1)
    got = spread(block, ("zh", "zl"), 16).reshape(2, 8, 8, width + 128)
    sums = jnp.sum(got[..., :width].astype(f32), axis=1)
    sums = (sums[..., :half] + sums[..., half:]).astype(bf16)
    pieces = got[:, :, :5, width:].reshape(2, 2, 4, half).astype(f32)
    slot_pair = pieces[:, 0] + pieces[:, 1]
    dots = jnp.sum(sums[:, 4:].astype(f32) * slot_pair, axis=2)
    dots = jnp.stack(split(dots, 3), axis=-1)
    dots = jnp.pad(dots, ((0, 0), (4, 0), (0, 125)))
    block = jnp.concatenate([sums, dots], axis=2).reshape(16, half + 128)
    got = spread(block, ("x", "y"), 16).reshape(16, 2, 2, 4, half + 128)
    got = got.transpose(2, 1, 0, 3, 4).reshape(256, half + 128)
    back = lax.ppermute(got, "core", swap)
    rows = whole(got[:, :half], back[:, :half])
    slot_out, grad_slot_in = rows[:128], rows[128:]
    slot_dot = jnp.sum(
        got[128:, half : half + 3].astype(f32) + back[128:, half : half + 3].astype(f32),
        axis=1,
    )

    grad_comb = contract(slot_out, cotangent_t, 1, 0)
    grad_disp = contract(grad_slot_in, patches_t, 1, 0)
    patch_dot = jnp.sum(comb_prob * grad_comb, axis=0)
    grad_logits = disp_prob * (grad_disp - slot_dot[:, None]) + comb_prob * (
        grad_comb - patch_dot[None, :]
    )
    scaled = (grad_logits * scale).astype(bf16)

    own_scaled = lax.dynamic_slice_in_dim(scaled, 4 * expert, 4, 0)
    router_part = contract(own_scaled, patches_t, 1, 1)
    router_part = router_part + lax.ppermute(router_part, "core", swap)
    got = spread(router_part.astype(bf16).reshape(8, half), "zl", 8)
    grad_router = jnp.sum(got.astype(f32), axis=0).astype(bf16).reshape(4, width)

    def tokens(array):
        return lax.dynamic_slice_in_dim(array, 8 * expert, 8, 1)

    mixed = contract(tokens(combine), slot_out, 0, 0).astype(bf16)
    grad_patches = contract(tokens(dispatch), grad_slot_in, 0, 0) + contract(
        tokens(scaled), router_all, 0, 0
    )
    return (mixed, grad_patches.astype(bf16), grad_router, grad_w_in, grad_w_out)


def solution(mesh):
    fine = Mesh(mesh.devices.reshape(8, 2, 2, 4, 4), ("zl", "core", "zh", "x", "y"))
    tok, exp = ("zl", "core"), ("zh", "x", "y")
    return jax.shard_map(
        body,
        mesh=fine,
        in_specs=(
            P(tok, exp),
            P(exp, None),
            P(exp, tok, None),
            P(exp, tok, None),
            P(tok, exp),
        ),
        out_specs=(
            P(tok + exp, None),
            P(tok + exp, None),
            P(exp, None),
            P(exp, tok, None),
            P(exp, tok, None),
        ),
        check_vma=False,
    )
```

time: 160 us -> 181 us (1.13)
  blocking collectives: 52.4 us -> 22.2 us
  starting transfers between devices: 50.8 us -> 79.9 us
  waiting for transfers between devices: 34.1 us -> 54.2 us
  matrix products: 8.34 us -> 11.7 us
  other arithmetic: 4.48 us -> 2.5 us
    all_to_all x3 -> x1, blocking collectives: 52.4 us -> 22.2 us  [spread(): lax.all_to_all(jnp.broadcast_to(block[None], (count,) + block.shape), axe...]
    all_to_all x2 -> x5, starting transfers between devices: 13.8 us -> 28.2 us  [spread(): lax.all_to_all(jnp.broadcast_to(block[None], (count,) + block.shape), axe...]
    all_to_all x0 -> x1, waiting for transfers between devices: none -> 12.5 us  [body(): lax.all_to_all(fan(lax.ppermute(packed, 'zh', swap), 16, 10 ** 11), ('x',...]
    all_to_all x2 -> x5, waiting for transfers between devices: 29.9 us -> 39.2 us  [spread(): lax.all_to_all(jnp.broadcast_to(block[None], (count,) + block.shape), axe...]
    ppermute x3 -> x6, starting transfers between devices: 28 us -> 36.1 us  [the longest x1 16.3 us: body(): lax.ppermute(packed, 'zh', swap)]
    all_to_all x0 -> x1, starting transfers between devices: none -> 3.77 us  [body(): lax.all_to_all(fan(lax.ppermute(packed, 'zh', swap), 16, 10 ** 11), ('x',...]
    dot_general x15, matrix products: 8.34 us -> 11.7 us  [contract(): lax.dot_general(left, right, (((left_dim,), (right_dim,)), ((), ())), pre...]
    ppermute x1, starting transfers between devices: 6.69 us -> 9.08 us  [body(): back = lax.ppermute(got, 'core', swap)]
  transfers between devices with their start and end apart: 7 -> 14, of which waited for: 7 -> 8; matrix products, arithmetic and copies ran while one was open for 4% -> 5% of each run, Pallas kernels for 0% -> 1%
where the time goes in v3:
time: 181 us; the launch traced here: 180 us
  starting transfers between devices  79.9 us (44%)
  waiting for transfers between devices  54.2 us (30%)
  blocking collectives  22.2 us (12%)
  matrix products  11.7 us (6%)
  local copies, waits for them, and re-layouts  7.72 us (4%)
  other arithmetic  2.5 us (1%)
    all_to_all x5, waiting for transfers between devices, spread(): lax.all_to_all(jnp.broadcast_to(block[None], (count,) + block.shape), axe...  39.2 us
    all_to_all x5, starting transfers between devices, spread(): lax.all_to_all(jnp.broadcast_to(block[None], (count,) + block.shape), axe...  28.2 us
    all_to_all x1, blocking collectives, spread(): lax.all_to_all(jnp.broadcast_to(block[None], (count,) + block.shape), axe...  22.2 us
    ppermute x1, starting transfers between devices, body(): lax.ppermute(packed, 'zh', swap)  16.3 us
    all_to_all x1, waiting for transfers between devices, body(): lax.all_to_all(fan(lax.ppermute(packed, 'zh', swap), 16, 10 ** 11), ('x',...  12.5 us
    dot_general x15, matrix products, contract(): lax.dot_general(left, right, (((left_dim,), (right_dim,)), ((), ())), pre...  11.7 us
    ppermute x1, starting transfers between devices, body(): full = whole(halves, lax.ppermute(halves, 'core', swap))  9.54 us
    ppermute x1, starting transfers between devices, body(): back = lax.ppermute(got, 'core', swap)  9.08 us
  transfers between devices with their start and end apart: 14, of which 8 were waited for; matrix products, arithmetic and copies ran while one was open for 5% of the time, Pallas kernels for 1%

profile of v3, /device:TPU:1, one launch (start us, length us, event | category | flops | bytes accessed | tf_op | source)
XLA Modules:
  0.0 180.3 jit_solution(10349399815486478940)
XLA Ops:
  1.4 1.5 concatenate.46
  2.9 16.3 %collective-permute-start = (bf16[100,256]{1,0:T(8,128)(2,1)S(1)}, bf16[100,256]{1,0:T(8,128)(2,1)S(1)}, u32[]{:S(2)}, u32[]{:S(2)}) collective-permute-start(bf16[100,256]{1,0:T(8,128)(2,1)S(1)} %concatenate.46), channel_id=1, source_target_pairs={{0,16},{16,0},{1,17},{17,1},{2,18},{18,2},{3,19},{19,3},{4,20},{20... | collective-permute-start | bytes 153608 | tf_op jit(solution)/shard_map/ppermute | solution.py:87
  19.2 1.0 broadcast_in_dim.20
  20.2 6.8 %all-to-all-start = ((bf16[16,100,256]{2,1,0:T(8,128)(2,1)}), bf16[16,100,256]{2,1,0:T(8,128)(2,1)S(1)}, u32[]{:S(2)}, u32[]{:S(2)}) async-start(bf16[16,100,256]{2,1,0:T(8,128)(2,1)} %broadcast_in_dim.20), calls=%async_computation | async-start | bytes 1703936 | tf_op jit(solution)/shard_map/all_to_all | solution.py:45
  26.9 1.0 shard_map.92
  27.9 12.4 %all-to-all-done = bf16[16,100,256]{2,1,0:T(8,128)(2,1)S(1)} async-done(((bf16[16,100,256]{2,1,0:T(8,128)(2,1)}), bf16[16,100,256]{2,1,0:T(8,128)(2,1)S(1)}, u32[]{:S(2)}, u32[]{:S(2)}) %all-to-all-start) | async-done | bytes 819232 | tf_op jit(solution)/shard_map/all_to_all | solution.py:45
  40.3 3.8 %all-to-all-start.1 = ((bf16[16,100,256]{2,1,0:T(8,128)(2,1)}), bf16[16,100,256]{2,1,0:T(8,128)(2,1)S(1)}, u32[]{:S(2)}, u32[]{:S(2)}) async-start(bf16[16,100,256]{2,1,0:T(8,128)(2,1)} %shard_map.92), calls=%async_computation.1 | async-start | bytes 1703936 | tf_op jit(solution)/shard_map/all_to_all | solution.py:87
  44.0 12.5 %all-to-all-done.1 = bf16[16,100,256]{2,1,0:T(8,128)(2,1)S(1)} async-done(((bf16[16,100,256]{2,1,0:T(8,128)(2,1)}), bf16[16,100,256]{2,1,0:T(8,128)(2,1)S(1)}, u32[]{:S(2)}, u32[]{:S(2)}) %all-to-all-start.1) | async-done | bytes 819232 | tf_op jit(solution)/shard_map/all_to_all | solution.py:87
  58.5 8.4 %all-to-all-start.2 = ((bf16[16,8,128]{2,1,0:T(8,128)(2,1)}), bf16[16,8,128]{2,1,0:T(8,128)(2,1)S(1)}, u32[]{:S(2)}, u32[]{:S(2)}) async-start(bf16[16,8,128]{2,1,0:T(8,128)(2,1)} %broadcast_in_dim.21), calls=%async_computation.2 | async-start | bytes 65536 | tf_op jit(solution)/shard_map/all_to_all | solution.py:45
  66.9 9.8 %all-to-all-done.2 = bf16[16,8,128]{2,1,0:T(8,128)(2,1)S(1)} async-done(((bf16[16,8,128]{2,1,0:T(8,128)(2,1)}), bf16[16,8,128]{2,1,0:T(8,128)(2,1)S(1)}, u32[]{:S(2)}, u32[]{:S(2)}) %all-to-all-start.2) | async-done | bytes 32800 | tf_op jit(solution)/shard_map/all_to_all | solution.py:45
  77.7 2.8 %collective-permute-start.1 = (f32[12,640]{1,0:T(8,128)S(1)}, f32[12,640]{1,0:T(8,128)S(1)}, u32[]{:S(2)}, u32[]{:S(2)}) collective-permute-start(f32[12,640]{1,0:T(8,128)S(1)} %fusion.24), channel_id=1, source_target_pairs={{0,32},{32,0},{1,33},{33,1},{2,34},{34,2},{3,35},{35,3},{4,36},{36... | collective-permute-start | bytes 92168 | tf_op jit(solution)/shard_map/ppermute | solution.py:125
  82.2 3.4 %all-to-all-start.3 = ((bf16[8,20,640]{2,1,0:T(8,128)(2,1)}), bf16[8,20,640]{2,1,0:T(8,128)(2,1)S(1)}, u32[]{:S(2)}, u32[]{:S(2)}) async-start(bf16[8,20,640]{2,1,0:T(8,128)(2,1)} %broadcast_in_dim.22), calls=%async_computation.3 | async-start | bytes 491520 | tf_op jit(solution)/shard_map/all_to_all | solution.py:45
  86.4 2.2 %collective-permute-start.2 = (bf16[320,640]{1,0:T(8,128)(2,1)}, bf16[320,640]{1,0:T(8,128)(2,1)}, u32[]{:S(2)}, u32[]{:S(2)}) collective-permute-start(bf16[320,640]{1,0:T(8,128)(2,1)} %get-tuple-element.20), channel_id=1, source_target_pairs={{0,32},{32,0},{1,33},{33,1},{2,34},{34,2},{3,35},{35,3},{4,36},{36... | collective-permute-start | bytes 1228808 | tf_op jit(solution)/shard_map/ppermute | solution.py:135
  88.8 2.1 %collective-permute-start.3 = (bf16[320,640]{1,0:T(8,128)(2,1)S(1)}, bf16[320,640]{1,0:T(8,128)(2,1)}, u32[]{:S(2)}, u32[]{:S(2)}) collective-permute-start(bf16[320,640]{1,0:T(8,128)(2,1)S(1)} %get-tuple-element.18), channel_id=1, source_target_pairs={{0,32},{32,0},{1,33},{33,1},{2,34},{34,2},{3,35},{35,3},{4,36},{36... | collective-permute-start | bytes 1228808 | tf_op jit(solution)/shard_map/ppermute | solution.py:137
  90.9 8.8 %all-to-all-done.3 = bf16[8,20,640]{2,1,0:T(8,128)(2,1)S(1)} async-done(((bf16[8,20,640]{2,1,0:T(8,128)(2,1)}), bf16[8,20,640]{2,1,0:T(8,128)(2,1)S(1)}, u32[]{:S(2)}, u32[]{:S(2)}) %all-to-all-start.3) | async-done | bytes 204832 | tf_op jit(solution)/shard_map/all_to_all | solution.py:45
  99.8 1.3 fusion.10
  101.1 1.4 fusion.8
  102.7 4.0 %collective-permute-start.4 = (f32[8,640]{1,0:T(8,128)S(1)}, f32[8,640]{1,0:T(8,128)S(1)}, u32[]{:S(2)}, u32[]{:S(2)}) collective-permute-start(f32[8,640]{1,0:T(8,128)S(1)} %pad_maximum_fusion.14), channel_id=1, source_target_pairs={{0,32},{32,0},{1,33},{33,1},{2,34},{34,2},{3,35},{35,3},{4,36},{36... | collective-permute-start | bytes 61448 | tf_op jit(solution)/shard_map/ppermute | solution.py:142
  107.6 1.2 fusion.9
  108.8 1.2 fusion.7
  110.1 22.2 %all_to_all.35 = bf16[16,8,1408]{2,1,0:T(8,128)(2,1)S(1)} all-to-all(bf16[16,8,1408]{2,1,0:T(8,128)(2,1)S(1)} %broadcast_in_dim.23), channel_id=1, replica_groups=mesh['zl'=8,'core'=2,'zh'=2,'x'=4,'y'=4] {'zh','zl'}, dimensions={0} | all-to-all | bytes 720896 | tf_op jit(solution)/shard_map/all_to_all | solution.py:45
  133.5 3.6 %all-to-all-start.5 = ((bf16[16,16,768]{2,1,0:T(8,128)(2,1)}), bf16[16,16,768]{2,1,0:T(8,128)(2,1)S(1)}, u32[]{:S(2)}, u32[]{:S(2)}) async-start(bf16[16,16,768]{2,1,0:T(8,128)(2,1)} %broadcast_in_dim.25), calls=%async_computation.5 | async-start | bytes 786432 | tf_op jit(solution)/shard_map/all_to_all | solution.py:45
  137.0 9.5 %collective-permute-start.7 = (bf16[8,640]{1,0:T(8,128)(2,1)S(1)}, bf16[8,640]{1,0:T(8,128)(2,1)S(1)}, u32[]{:S(2)}, u32[]{:S(2)}) collective-permute-start(bf16[8,640]{1,0:T(8,128)(2,1)S(1)} %pad_maximum_fusion.18), channel_id=1, source_target_pairs={{0,32},{32,0},{1,33},{33,1},{2,34},{34,2},{3,35},{35,3},{4,36},{36... | collective-permute-start | bytes 30728 | tf_op jit(solution)/shard_map/ppermute | solution.py:151
  147.0 9.1 %collective-permute-start.5 = (bf16[256,768]{1,0:T(8,128)(2,1)S(1)}, bf16[256,768]{1,0:T(8,128)(2,1)S(1)}, u32[]{:S(2)}, u32[]{:S(2)}) collective-permute-start(bf16[256,768]{1,0:T(8,128)(2,1)S(1)} %reshape.174), channel_id=1, source_target_pairs={{0,32},{32,0},{1,33},{33,1},{2,34},{34,2},{3,35},{35,3},{4,36},{36... | collective-permute-start | bytes 1179656 | tf_op jit(solution)/shard_map/ppermute | solution.py:171
  156.2 1.3 fusion
  157.5 1.3 fusion.1
  159.8 1.9 %collective-permute-start.6 = (f32[4,1280]{1,0:T(4,128)S(1)}, f32[4,1280]{1,0:T(4,128)S(1)}, u32[]{:S(2)}, u32[]{:S(2)}) collective-permute-start(f32[4,1280]{1,0:T(4,128)S(1)} %fusion.76), channel_id=1, source_target_pairs={{0,32},{32,0},{1,33},{33,1},{2,34},{34,2},{3,35},{35,3},{4,36},{36... | collective-permute-start | bytes 61448 | tf_op jit(solution)/shard_map/ppermute | solution.py:189
  162.1 0.9 collective-permute-done.6
  163.6 6.1 %all-to-all-start.6 = ((bf16[8,8,640]{2,1,0:T(8,128)(2,1)}), bf16[8,8,640]{2,1,0:T(8,128)(2,1)S(1)}, u32[]{:S(2)}, u32[]{:S(2)}) async-start(bf16[8,8,640]{2,1,0:T(8,128)(2,1)} %broadcast_in_dim.27), calls=%async_computation.6 | async-start | bytes 163840 | tf_op jit(solution)/shard_map/all_to_all | solution.py:45
  169.7 0.9 convolution_convert_fusion.2
  170.6 0.9 fusion.2
  171.5 8.2 %all-to-all-done.6 = bf16[8,8,640]{2,1,0:T(8,128)(2,1)S(1)} async-done(((bf16[8,8,640]{2,1,0:T(8,128)(2,1)}), bf16[8,8,640]{2,1,0:T(8,128)(2,1)S(1)}, u32[]{:S(2)}, u32[]{:S(2)}) %all-to-all-start.6) | async-done | bytes 81952 | tf_op jit(solution)/shard_map/all_to_all | solution.py:45
  (82 shorter events, 11.4 us)
Async XLA Ops:
  2.9 24.0 %collective-permute-start = (bf16[100,256]{1,0:T(8,128)(2,1)S(1)}, bf16[100,256]{1,0:T(8,128)(2,1)S(1)}, u32[]{:S(2)}, u32[]{:S(2)}) collective-permute-start(bf16[100,256]{1,0:T(8,128)(2,1)S(1)} %concatenate.46), channel_id=1, source_target_pairs={{0,16},{16,0},{1,17},{17,1},{2,18},{18,2},{3,19},{19,3},{4,20},{20... | collective-permute-start | bytes 153608 | tf_op jit(solution)/shard_map/ppermute | solution.py:87
  20.2 20.1 %all-to-all-start = ((bf16[16,100,256]{2,1,0:T(8,128)(2,1)}), bf16[16,100,256]{2,1,0:T(8,128)(2,1)S(1)}, u32[]{:S(2)}, u32[]{:S(2)}) async-start(bf16[16,100,256]{2,1,0:T(8,128)(2,1)} %broadcast_in_dim.20), calls=%async_computation | async-start | bytes 1703936 | tf_op jit(solution)/shard_map/all_to_all | solution.py:45
  40.3 16.3 %all-to-all-start.1 = ((bf16[16,100,256]{2,1,0:T(8,128)(2,1)}), bf16[16,100,256]{2,1,0:T(8,128)(2,1)S(1)}, u32[]{:S(2)}, u32[]{:S(2)}) async-start(bf16[16,100,256]{2,1,0:T(8,128)(2,1)} %shard_map.92), calls=%async_computation.1 | async-start | bytes 1703936 | tf_op jit(solution)/shard_map/all_to_all | solution.py:87
  58.5 18.3 %all-to-all-start.2 = ((bf16[16,8,128]{2,1,0:T(8,128)(2,1)}), bf16[16,8,128]{2,1,0:T(8,128)(2,1)S(1)}, u32[]{:S(2)}, u32[]{:S(2)}) async-start(bf16[16,8,128]{2,1,0:T(8,128)(2,1)} %broadcast_in_dim.21), calls=%async_computation.2 | async-start | bytes 65536 | tf_op jit(solution)/shard_map/all_to_all | solution.py:45
  77.4 8.2 %copy-start = (bf16[1,320,1280]{2,1,0:T(8,128)(2,1)S(1)}, bf16[1,320,1280]{2,1,0:T(8,128)(2,1)}, u32[]{:S(2)}) copy-start(bf16[1,320,1280]{2,1,0:T(8,128)(2,1)} %param.7) | copy-start | bytes 2457604
  77.7 3.6 %collective-permute-start.1 = (f32[12,640]{1,0:T(8,128)S(1)}, f32[12,640]{1,0:T(8,128)S(1)}, u32[]{:S(2)}, u32[]{:S(2)}) collective-permute-start(f32[12,640]{1,0:T(8,128)S(1)} %fusion.24), channel_id=1, source_target_pairs={{0,32},{32,0},{1,33},{33,1},{2,34},{34,2},{3,35},{35,3},{4,36},{36... | collective-permute-start | bytes 92168 | tf_op jit(solution)/shard_map/ppermute | solution.py:125
  82.2 17.5 %all-to-all-start.3 = ((bf16[8,20,640]{2,1,0:T(8,128)(2,1)}), bf16[8,20,640]{2,1,0:T(8,128)(2,1)S(1)}, u32[]{:S(2)}, u32[]{:S(2)}) async-start(bf16[8,20,640]{2,1,0:T(8,128)(2,1)} %broadcast_in_dim.22), calls=%async_computation.3 | async-start | bytes 491520 | tf_op jit(solution)/shard_map/all_to_all | solution.py:45
  85.6 3.1 %copy-start.1 = (bf16[1,320,1280]{2,1,0:T(8,128)(2,1)S(1)}, bf16[1,320,1280]{2,1,0:T(8,128)(2,1)}, u32[]{:S(2)}) copy-start(bf16[1,320,1280]{2,1,0:T(8,128)(2,1)} %param.8) | copy-start | bytes 2457604
  86.4 13.4 %collective-permute-start.2 = (bf16[320,640]{1,0:T(8,128)(2,1)}, bf16[320,640]{1,0:T(8,128)(2,1)}, u32[]{:S(2)}, u32[]{:S(2)}) collective-permute-start(bf16[320,640]{1,0:T(8,128)(2,1)} %get-tuple-element.20), channel_id=1, source_target_pairs={{0,32},{32,0},{1,33},{33,1},{2,34},{34,2},{3,35},{35,3},{4,36},{36... | collective-permute-start | bytes 1228808 | tf_op jit(solution)/shard_map/ppermute | solution.py:135
  88.8 12.4 %collective-permute-start.3 = (bf16[320,640]{1,0:T(8,128)(2,1)S(1)}, bf16[320,640]{1,0:T(8,128)(2,1)}, u32[]{:S(2)}, u32[]{:S(2)}) collective-permute-start(bf16[320,640]{1,0:T(8,128)(2,1)S(1)} %get-tuple-element.18), channel_id=1, source_target_pairs={{0,32},{32,0},{1,33},{33,1},{2,34},{34,2},{3,35},{35,3},{4,36},{36... | collective-permute-start | bytes 1228808 | tf_op jit(solution)/shard_map/ppermute | solution.py:137
  102.7 4.9 %collective-permute-start.4 = (f32[8,640]{1,0:T(8,128)S(1)}, f32[8,640]{1,0:T(8,128)S(1)}, u32[]{:S(2)}, u32[]{:S(2)}) collective-permute-start(f32[8,640]{1,0:T(8,128)S(1)} %pad_maximum_fusion.14), channel_id=1, source_target_pairs={{0,32},{32,0},{1,33},{33,1},{2,34},{34,2},{3,35},{35,3},{4,36},{36... | collective-permute-start | bytes 61448 | tf_op jit(solution)/shard_map/ppermute | solution.py:142
  133.5 13.1 %all-to-all-start.5 = ((bf16[16,16,768]{2,1,0:T(8,128)(2,1)}), bf16[16,16,768]{2,1,0:T(8,128)(2,1)S(1)}, u32[]{:S(2)}, u32[]{:S(2)}) async-start(bf16[16,16,768]{2,1,0:T(8,128)(2,1)} %broadcast_in_dim.25), calls=%async_computation.5 | async-start | bytes 786432 | tf_op jit(solution)/shard_map/all_to_all | solution.py:45
  137.0 19.1 %collective-permute-start.7 = (bf16[8,640]{1,0:T(8,128)(2,1)S(1)}, bf16[8,640]{1,0:T(8,128)(2,1)S(1)}, u32[]{:S(2)}, u32[]{:S(2)}) collective-permute-start(bf16[8,640]{1,0:T(8,128)(2,1)S(1)} %pad_maximum_fusion.18), channel_id=1, source_target_pairs={{0,32},{32,0},{1,33},{33,1},{2,34},{34,2},{3,35},{35,3},{4,36},{36... | collective-permute-start | bytes 30728 | tf_op jit(solution)/shard_map/ppermute | solution.py:151
  147.0 11.8 %collective-permute-start.5 = (bf16[256,768]{1,0:T(8,128)(2,1)S(1)}, bf16[256,768]{1,0:T(8,128)(2,1)S(1)}, u32[]{:S(2)}, u32[]{:S(2)}) collective-permute-start(bf16[256,768]{1,0:T(8,128)(2,1)S(1)} %reshape.174), channel_id=1, source_target_pairs={{0,32},{32,0},{1,33},{33,1},{2,34},{34,2},{3,35},{35,3},{4,36},{36... | collective-permute-start | bytes 1179656 | tf_op jit(solution)/shard_map/ppermute | solution.py:171
  159.8 3.1 %collective-permute-start.6 = (f32[4,1280]{1,0:T(4,128)S(1)}, f32[4,1280]{1,0:T(4,128)S(1)}, u32[]{:S(2)}, u32[]{:S(2)}) collective-permute-start(f32[4,1280]{1,0:T(4,128)S(1)} %fusion.76), channel_id=1, source_target_pairs={{0,32},{32,0},{1,33},{33,1},{2,34},{34,2},{3,35},{35,3},{4,36},{36... | collective-permute-start | bytes 61448 | tf_op jit(solution)/shard_map/ppermute | solution.py:189
  163.6 16.1 %all-to-all-start.6 = ((bf16[8,8,640]{2,1,0:T(8,128)(2,1)}), bf16[8,8,640]{2,1,0:T(8,128)(2,1)S(1)}, u32[]{:S(2)}, u32[]{:S(2)}) async-start(bf16[8,8,640]{2,1,0:T(8,128)(2,1)} %broadcast_in_dim.27), calls=%async_computation.6 | async-start | bytes 163840 | tf_op jit(solution)/shard_map/all_to_all | solution.py:45

commit v4 on v3

--- a/solution.py
+++ b/solution.py
@@ -132,12 +132,21 @@
     halves = jnp.concatenate([slot_half, grad_half], axis=0).astype(bf16)
 
     rows = w_in.shape[1]
-    pair_in = jnp.concatenate([mine(w_in[0]), lax.ppermute(other(w_in[0]), "core", swap)], axis=0)
-    pair_out = jnp.concatenate(
-        [mine(w_out[0]), lax.ppermute(other(w_out[0]), "core", swap)], axis=0
-    )
+    in_own, in_far = mine(w_in[0]), lax.ppermute(other(w_in[0]), "core", swap)
+    out_own, out_far = mine(w_out[0]), lax.ppermute(other(w_out[0]), "core", swap)
+
+    def units(rows_of, own_part, far_part):
+        return jnp.concatenate(
+            [contract(rows_of, own_part, 1, 1), contract(rows_of, far_part, 1, 1)], axis=1
+        )
+
+    def features(units_of, own_part, far_part):
+        return contract(units_of[:, :rows], own_part, 1, 0) + contract(
+            units_of[:, rows:], far_part, 1, 0
+        )
+
     pre = jnp.concatenate(
-        [contract(halves[:4], pair_in, 1, 1), contract(halves[4:], pair_out, 1, 1)], axis=0
+        [units(halves[:4], in_own, in_far), units(halves[4:], out_own, out_far)], axis=0
     )
     pre = pre + lax.ppermute(
         jnp.concatenate([pre[:, rows:], pre[:, :rows]], axis=1), "core", swap
@@ -146,7 +155,7 @@
     hidden = gelu_value(pre_act).astype(bf16)
     grad_pre = (grad_hidden * gelu_slope(pre_act)).astype(bf16)
     parts = jnp.concatenate(
-        [contract(hidden, pair_out, 1, 0), contract(grad_pre, pair_in, 1, 0)], axis=0
+        [features(hidden, out_own, out_far), features(grad_pre, in_own, in_far)], axis=0
     )
     full = whole(halves, lax.ppermute(halves, "core", swap))
     grad_w_out = contract(hidden[:, :rows], full[4:], 0, 0).astype(bf16)[None]

time: 181 us -> 184 us (1.017)
  other arithmetic: 2.5 us -> 6.01 us
  matrix products: 11.7 us -> 9.2 us
  local copies, waits for them, and re-layouts: 7.72 us -> 9.73 us
    dot_general x15 -> x19, matrix products: 11.7 us -> 9.2 us  [contract(): lax.dot_general(left, right, (((left_dim,), (right_dim,)), ((), ())), pre...]
    unnamed x6 -> x44, local copies, waits for them, and re-layouts: 0.21 us -> 2.09 us
  transfers between devices with their start and end apart: 14 -> 14, of which waited for: 8 -> 8; matrix products, arithmetic and copies ran while one was open for 5% -> 6% of each run, Pallas kernels for 1% -> 1%
where the time goes in v4:
time: 184 us; the launch traced here: 183 us
  starting transfers between devices  80 us (43%)
  waiting for transfers between devices  53.1 us (29%)
  blocking collectives  22.2 us (12%)
  local copies, waits for them, and re-layouts  9.73 us (5%)
  matrix products  9.2 us (5%)
  other arithmetic  6.01 us (3%)
    all_to_all x5, waiting for transfers between devices, spread(): lax.all_to_all(jnp.broadcast_to(block[None], (count,) + block.shape), axe...  38.5 us
    all_to_all x5, starting transfers between devices, spread(): lax.all_to_all(jnp.broadcast_to(block[None], (count,) + block.shape), axe...  28.2 us
    all_to_all x1, blocking collectives, spread(): lax.all_to_all(jnp.broadcast_to(block[None], (count,) + block.shape), axe...  22.2 us
    ppermute x1, starting transfers between devices, body(): lax.ppermute(packed, 'zh', swap)  16.3 us
    all_to_all x1, waiting for transfers between devices, body(): lax.all_to_all(fan(lax.ppermute(packed, 'zh', swap), 16, 10 ** 11), ('x',...  12.5 us
    ppermute x1, starting transfers between devices, body(): full = whole(halves, lax.ppermute(halves, 'core', swap))  9.54 us
    dot_general x19, matrix products, contract(): lax.dot_general(left, right, (((left_dim,), (right_dim,)), ((), ())), pre...  9.2 us
    ppermute x1, starting transfers between devices, body(): back = lax.ppermute(got, 'core', swap)  9.08 us
  transfers between devices with their start and end apart: 14, of which 8 were waited for; matrix products, arithmetic and copies ran while one was open for 6% of the time, Pallas kernels for 1%

profile of v4, /device:TPU:1, one launch (start us, length us, event | category | flops | bytes accessed | tf_op | source)
XLA Modules:
  0.0 182.6 jit_solution(10403204721825851880)
XLA Ops:
  1.4 1.5 concatenate.46
  2.9 16.3 %collective-permute-start = (bf16[100,256]{1,0:T(8,128)(2,1)S(1)}, bf16[100,256]{1,0:T(8,128)(2,1)S(1)}, u32[]{:S(2)}, u32[]{:S(2)}) collective-permute-start(bf16[100,256]{1,0:T(8,128)(2,1)S(1)} %concatenate.46), channel_id=1, source_target_pairs={{0,16},{16,0},{1,17},{17,1},{2,18},{18,2},{3,19},{19,3},{4,20},{20... | collective-permute-start | bytes 153608 | tf_op jit(solution)/shard_map/ppermute | solution.py:87
  19.2 1.0 broadcast_in_dim.20
  20.2 6.8 %all-to-all-start = ((bf16[16,100,256]{2,1,0:T(8,128)(2,1)}), bf16[16,100,256]{2,1,0:T(8,128)(2,1)S(1)}, u32[]{:S(2)}, u32[]{:S(2)}) async-start(bf16[16,100,256]{2,1,0:T(8,128)(2,1)} %broadcast_in_dim.20), calls=%async_computation | async-start | bytes 1703936 | tf_op jit(solution)/shard_map/all_to_all | solution.py:45
  27.0 1.0 shard_map.92
  27.9 12.4 %all-to-all-done = bf16[16,100,256]{2,1,0:T(8,128)(2,1)S(1)} async-done(((bf16[16,100,256]{2,1,0:T(8,128)(2,1)}), bf16[16,100,256]{2,1,0:T(8,128)(2,1)S(1)}, u32[]{:S(2)}, u32[]{:S(2)}) %all-to-all-start) | async-done | bytes 819232 | tf_op jit(solution)/shard_map/all_to_all | solution.py:45
  40.3 3.8 %all-to-all-start.1 = ((bf16[16,100,256]{2,1,0:T(8,128)(2,1)}), bf16[16,100,256]{2,1,0:T(8,128)(2,1)S(1)}, u32[]{:S(2)}, u32[]{:S(2)}) async-start(bf16[16,100,256]{2,1,0:T(8,128)(2,1)} %shard_map.92), calls=%async_computation.1 | async-start | bytes 1703936 | tf_op jit(solution)/shard_map/all_to_all | solution.py:87
  44.1 12.5 %all-to-all-done.1 = bf16[16,100,256]{2,1,0:T(8,128)(2,1)S(1)} async-done(((bf16[16,100,256]{2,1,0:T(8,128)(2,1)}), bf16[16,100,256]{2,1,0:T(8,128)(2,1)S(1)}, u32[]{:S(2)}, u32[]{:S(2)}) %all-to-all-start.1) | async-done | bytes 819232 | tf_op jit(solution)/shard_map/all_to_all | solution.py:87
  58.5 8.4 %all-to-all-start.2 = ((bf16[16,8,128]{2,1,0:T(8,128)(2,1)}), bf16[16,8,128]{2,1,0:T(8,128)(2,1)S(1)}, u32[]{:S(2)}, u32[]{:S(2)}) async-start(bf16[16,8,128]{2,1,0:T(8,128)(2,1)} %broadcast_in_dim.21), calls=%async_computation.2 | async-start | bytes 65536 | tf_op jit(solution)/shard_map/all_to_all | solution.py:45
  67.0 9.8 %all-to-all-done.2 = bf16[16,8,128]{2,1,0:T(8,128)(2,1)S(1)} async-done(((bf16[16,8,128]{2,1,0:T(8,128)(2,1)}), bf16[16,8,128]{2,1,0:T(8,128)(2,1)S(1)}, u32[]{:S(2)}, u32[]{:S(2)}) %all-to-all-start.2) | async-done | bytes 32800 | tf_op jit(solution)/shard_map/all_to_all | solution.py:45
  78.3 2.8 %collective-permute-start.1 = (f32[12,640]{1,0:T(8,128)S(1)}, f32[12,640]{1,0:T(8,128)S(1)}, u32[]{:S(2)}, u32[]{:S(2)}) collective-permute-start(f32[12,640]{1,0:T(8,128)S(1)} %fusion.24), channel_id=1, source_target_pairs={{0,32},{32,0},{1,33},{33,1},{2,34},{34,2},{3,35},{35,3},{4,36},{36... | collective-permute-start | bytes 92168 | tf_op jit(solution)/shard_map/ppermute | solution.py:125
  81.1 0.8 collective-permute-done.1
  82.8 3.4 %all-to-all-start.3 = ((bf16[8,20,640]{2,1,0:T(8,128)(2,1)}), bf16[8,20,640]{2,1,0:T(8,128)(2,1)S(1)}, u32[]{:S(2)}, u32[]{:S(2)}) async-start(bf16[8,20,640]{2,1,0:T(8,128)(2,1)} %broadcast_in_dim.22), calls=%async_computation.3 | async-start | bytes 491520 | tf_op jit(solution)/shard_map/all_to_all | solution.py:45
  87.0 2.2 %collective-permute-start.3 = (bf16[320,640]{1,0:T(8,128)(2,1)}, bf16[320,640]{1,0:T(8,128)(2,1)S(1)}, u32[]{:S(2)}, u32[]{:S(2)}) collective-permute-start(bf16[320,640]{1,0:T(8,128)(2,1)} %broadcast_select_fusion), channel_id=1, source_target_pairs={{0,32},{32,0},{1,33},{33,1},{2,34},{34,2},{3,35},{35,3},{4,36},{36... | collective-permute-start | bytes 1228808 | tf_op jit(solution)/shard_map/ppermute | solution.py:136
  90.1 2.1 %collective-permute-start.2 = (bf16[320,640]{1,0:T(8,128)(2,1)}, bf16[320,640]{1,0:T(8,128)(2,1)S(1)}, u32[]{:S(2)}, u32[]{:S(2)}) collective-permute-start(bf16[320,640]{1,0:T(8,128)(2,1)} %broadcast_select_fusion.2), channel_id=1, source_target_pairs={{0,32},{32,0},{1,33},{33,1},{2,34},{34,2},{3,35},{35,3},{4,36},{36... | collective-permute-start | bytes 1228808 | tf_op jit(solution)/shard_map/ppermute | solution.py:135
  92.2 8.1 %all-to-all-done.3 = bf16[8,20,640]{2,1,0:T(8,128)(2,1)S(1)} async-done(((bf16[8,20,640]{2,1,0:T(8,128)(2,1)}), bf16[8,20,640]{2,1,0:T(8,128)(2,1)S(1)}, u32[]{:S(2)}, u32[]{:S(2)}) %all-to-all-start.3) | async-done | bytes 204832 | tf_op jit(solution)/shard_map/all_to_all | solution.py:45
  101.0 1.3 fusion.13
  104.4 4.0 %collective-permute-start.4 = (f32[8,640]{1,0:T(8,128)}, f32[8,640]{1,0:T(8,128)}, u32[]{:S(2)}, u32[]{:S(2)}) collective-permute-start(f32[8,640]{1,0:T(8,128)} %pad_maximum_fusion.7), channel_id=1, source_target_pairs={{0,32},{32,0},{1,33},{33,1},{2,34},{34,2},{3,35},{35,3},{4,36},{36... | collective-permute-start | bytes 61448 | tf_op jit(solution)/shard_map/ppermute | solution.py:151
  108.4 0.8 fusion.71
  109.6 0.8 fusion.117
  111.6 22.2 %all_to_all.35 = bf16[16,8,1408]{2,1,0:T(8,128)(2,1)S(1)} all-to-all(bf16[16,8,1408]{2,1,0:T(8,128)(2,1)S(1)} %broadcast_in_dim.23), channel_id=1, replica_groups=mesh['zl'=8,'core'=2,'zh'=2,'x'=4,'y'=4] {'zh','zl'}, dimensions={0} | all-to-all | bytes 720896 | tf_op jit(solution)/shard_map/all_to_all | solution.py:45
  134.9 3.6 %all-to-all-start.5 = ((bf16[16,16,768]{2,1,0:T(8,128)(2,1)}), bf16[16,16,768]{2,1,0:T(8,128)(2,1)S(1)}, u32[]{:S(2)}, u32[]{:S(2)}) async-start(bf16[16,16,768]{2,1,0:T(8,128)(2,1)} %broadcast_in_dim.25), calls=%async_computation.5 | async-start | bytes 786432 | tf_op jit(solution)/shard_map/all_to_all | solution.py:45
  138.5 9.5 %collective-permute-start.7 = (bf16[8,640]{1,0:T(8,128)(2,1)S(1)}, bf16[8,640]{1,0:T(8,128)(2,1)S(1)}, u32[]{:S(2)}, u32[]{:S(2)}) collective-permute-start(bf16[8,640]{1,0:T(8,128)(2,1)S(1)} %pad_maximum_fusion.11), channel_id=1, source_target_pairs={{0,32},{32,0},{1,33},{33,1},{2,34},{34,2},{3,35},{35,3},{4,36},{36... | collective-permute-start | bytes 30728 | tf_op jit(solution)/shard_map/ppermute | solution.py:160
  148.5 9.1 %collective-permute-start.5 = (bf16[256,768]{1,0:T(8,128)(2,1)S(1)}, bf16[256,768]{1,0:T(8,128)(2,1)S(1)}, u32[]{:S(2)}, u32[]{:S(2)}) collective-permute-start(bf16[256,768]{1,0:T(8,128)(2,1)S(1)} %reshape.174), channel_id=1, source_target_pairs={{0,32},{32,0},{1,33},{33,1},{2,34},{34,2},{3,35},{35,3},{4,36},{36... | collective-permute-start | bytes 1179656 | tf_op jit(solution)/shard_map/ppermute | solution.py:180
  157.6 1.3 fusion
  159.0 1.3 fusion.1
  161.9 2.1 %collective-permute-start.6 = (f32[4,1280]{1,0:T(4,128)S(1)}, f32[4,1280]{1,0:T(4,128)S(1)}, u32[]{:S(2)}, u32[]{:S(2)}) collective-permute-start(f32[4,1280]{1,0:T(4,128)S(1)} %fusion.77), channel_id=1, source_target_pairs={{0,32},{32,0},{1,33},{33,1},{2,34},{34,2},{3,35},{35,3},{4,36},{36... | collective-permute-start | bytes 61448 | tf_op jit(solution)/shard_map/ppermute | solution.py:198
  164.3 0.9 collective-permute-done.6
  165.8 6.1 %all-to-all-start.6 = ((bf16[8,8,640]{2,1,0:T(8,128)(2,1)}), bf16[8,8,640]{2,1,0:T(8,128)(2,1)S(1)}, u32[]{:S(2)}, u32[]{:S(2)}) async-start(bf16[8,8,640]{2,1,0:T(8,128)(2,1)} %broadcast_in_dim.27), calls=%async_computation.6 | async-start | bytes 163840 | tf_op jit(solution)/shard_map/all_to_all | solution.py:45
  171.9 0.9 convolution_convert_fusion.2
  172.8 0.9 fusion.2
  173.7 8.2 %all-to-all-done.6 = bf16[8,8,640]{2,1,0:T(8,128)(2,1)S(1)} async-done(((bf16[8,8,640]{2,1,0:T(8,128)(2,1)}), bf16[8,8,640]{2,1,0:T(8,128)(2,1)S(1)}, u32[]{:S(2)}, u32[]{:S(2)}) %all-to-all-start.6) | async-done | bytes 81952 | tf_op jit(solution)/shard_map/all_to_all | solution.py:45
  (125 shorter events, 15.4 us)
Async XLA Ops:
  2.9 24.1 %collective-permute-start = (bf16[100,256]{1,0:T(8,128)(2,1)S(1)}, bf16[100,256]{1,0:T(8,128)(2,1)S(1)}, u32[]{:S(2)}, u32[]{:S(2)}) collective-permute-start(bf16[100,256]{1,0:T(8,128)(2,1)S(1)} %concatenate.46), channel_id=1, source_target_pairs={{0,16},{16,0},{1,17},{17,1},{2,18},{18,2},{3,19},{19,3},{4,20},{20... | collective-permute-start | bytes 153608 | tf_op jit(solution)/shard_map/ppermute | solution.py:87
  20.2 20.1 %all-to-all-start = ((bf16[16,100,256]{2,1,0:T(8,128)(2,1)}), bf16[16,100,256]{2,1,0:T(8,128)(2,1)S(1)}, u32[]{:S(2)}, u32[]{:S(2)}) async-start(bf16[16,100,256]{2,1,0:T(8,128)(2,1)} %broadcast_in_dim.20), calls=%async_computation | async-start | bytes 1703936 | tf_op jit(solution)/shard_map/all_to_all | solution.py:45
  40.3 16.3 %all-to-all-start.1 = ((bf16[16,100,256]{2,1,0:T(8,128)(2,1)}), bf16[16,100,256]{2,1,0:T(8,128)(2,1)S(1)}, u32[]{:S(2)}, u32[]{:S(2)}) async-start(bf16[16,100,256]{2,1,0:T(8,128)(2,1)} %shard_map.92), calls=%async_computation.1 | async-start | bytes 1703936 | tf_op jit(solution)/shard_map/all_to_all | solution.py:87
  57.6 20.0 %copy-start.17 = (f32[256]{0:T(256)}, f32[256]{0:T(256)S(1)}, u32[]{:S(2)}) copy-start(f32[256]{0:T(256)S(1)} %get-tuple-element.8) | copy-start | bytes 3076
  57.9 19.8 %copy-start.19 = (f32[256]{0:T(256)}, f32[256]{0:T(256)S(1)}, u32[]{:S(2)}) copy-start(f32[256]{0:T(256)S(1)} %get-tuple-element.6) | copy-start | bytes 3076
  58.5 18.3 %all-to-all-start.2 = ((bf16[16,8,128]{2,1,0:T(8,128)(2,1)}), bf16[16,8,128]{2,1,0:T(8,128)(2,1)S(1)}, u32[]{:S(2)}, u32[]{:S(2)}) async-start(bf16[16,8,128]{2,1,0:T(8,128)(2,1)} %broadcast_in_dim.21), calls=%async_computation.2 | async-start | bytes 65536 | tf_op jit(solution)/shard_map/all_to_all | solution.py:45
  77.1 1.3 copy-start.7
  78.0 8.2 %copy-start.3 = (bf16[1,320,1280]{2,1,0:T(8,128)(2,1)S(1)}, bf16[1,320,1280]{2,1,0:T(8,128)(2,1)}, u32[]{:S(2)}) copy-start(bf16[1,320,1280]{2,1,0:T(8,128)(2,1)} %param.8) | copy-start | bytes 2457604
  78.3 3.6 %collective-permute-start.1 = (f32[12,640]{1,0:T(8,128)S(1)}, f32[12,640]{1,0:T(8,128)S(1)}, u32[]{:S(2)}, u32[]{:S(2)}) collective-permute-start(f32[12,640]{1,0:T(8,128)S(1)} %fusion.24), channel_id=1, source_target_pairs={{0,32},{32,0},{1,33},{33,1},{2,34},{34,2},{3,35},{35,3},{4,36},{36... | collective-permute-start | bytes 92168 | tf_op jit(solution)/shard_map/ppermute | solution.py:125
  82.8 17.5 %all-to-all-start.3 = ((bf16[8,20,640]{2,1,0:T(8,128)(2,1)}), bf16[8,20,640]{2,1,0:T(8,128)(2,1)S(1)}, u32[]{:S(2)}, u32[]{:S(2)}) async-start(bf16[8,20,640]{2,1,0:T(8,128)(2,1)} %broadcast_in_dim.22), calls=%async_computation.3 | async-start | bytes 491520 | tf_op jit(solution)/shard_map/all_to_all | solution.py:45
  86.2 3.1 %copy-start = (bf16[1,320,1280]{2,1,0:T(8,128)(2,1)S(1)}, bf16[1,320,1280]{2,1,0:T(8,128)(2,1)}, u32[]{:S(2)}) copy-start(bf16[1,320,1280]{2,1,0:T(8,128)(2,1)} %param.7) | copy-start | bytes 2457604
  87.0 15.6 %collective-permute-start.3 = (bf16[320,640]{1,0:T(8,128)(2,1)}, bf16[320,640]{1,0:T(8,128)(2,1)S(1)}, u32[]{:S(2)}, u32[]{:S(2)}) collective-permute-start(bf16[320,640]{1,0:T(8,128)(2,1)} %broadcast_select_fusion), channel_id=1, source_target_pairs={{0,32},{32,0},{1,33},{33,1},{2,34},{34,2},{3,35},{35,3},{4,36},{36... | collective-permute-start | bytes 1228808 | tf_op jit(solution)/shard_map/ppermute | solution.py:136
  90.1 12.7 %collective-permute-start.2 = (bf16[320,640]{1,0:T(8,128)(2,1)}, bf16[320,640]{1,0:T(8,128)(2,1)S(1)}, u32[]{:S(2)}, u32[]{:S(2)}) collective-permute-start(bf16[320,640]{1,0:T(8,128)(2,1)} %broadcast_select_fusion.2), channel_id=1, source_target_pairs={{0,32},{32,0},{1,33},{33,1},{2,34},{34,2},{3,35},{35,3},{4,36},{36... | collective-permute-start | bytes 1228808 | tf_op jit(solution)/shard_map/ppermute | solution.py:135
  100.3 2.1 %copy-start.1 = (bf16[1,320,1280]{2,1,0:T(8,128)(2,1)S(1)}, bf16[1,320,1280]{2,1,0:T(8,128)(2,1)}, u32[]{:S(2)}) copy-start(bf16[1,320,1280]{2,1,0:T(8,128)(2,1)} %param.7) | copy-start | bytes 2457604
  102.3 0.7 copy-start.15
  102.4 8.1 %copy-start.2 = (bf16[1,320,1280]{2,1,0:T(8,128)(2,1)S(1)}, bf16[1,320,1280]{2,1,0:T(8,128)(2,1)}, u32[]{:S(2)}) copy-start(bf16[1,320,1280]{2,1,0:T(8,128)(2,1)} %param.7) | copy-start | bytes 2457604
  102.6 1.8 copy-start.16
  103.0 0.7 copy-start.10
  104.4 5.2 %collective-permute-start.4 = (f32[8,640]{1,0:T(8,128)}, f32[8,640]{1,0:T(8,128)}, u32[]{:S(2)}, u32[]{:S(2)}) collective-permute-start(f32[8,640]{1,0:T(8,128)} %pad_maximum_fusion.7), channel_id=1, source_target_pairs={{0,32},{32,0},{1,33},{33,1},{2,34},{34,2},{3,35},{35,3},{4,36},{36... | collective-permute-start | bytes 61448 | tf_op jit(solution)/shard_map/ppermute | solution.py:151
  108.4 2.2 %copy-start.4 = (bf16[1,320,1280]{2,1,0:T(8,128)(2,1)S(1)}, bf16[1,320,1280]{2,1,0:T(8,128)(2,1)}, u32[]{:S(2)}) copy-start(bf16[1,320,1280]{2,1,0:T(8,128)(2,1)} %param.8) | copy-start | bytes 2457604
  110.5 0.8 copy-start.11
  134.9 13.1 %all-to-all-start.5 = ((bf16[16,16,768]{2,1,0:T(8,128)(2,1)}), bf16[16,16,768]{2,1,0:T(8,128)(2,1)S(1)}, u32[]{:S(2)}, u32[]{:S(2)}) async-start(bf16[16,16,768]{2,1,0:T(8,128)(2,1)} %broadcast_in_dim.25), calls=%async_computation.5 | async-start | bytes 786432 | tf_op jit(solution)/shard_map/all_to_all | solution.py:45
  138.5 19.1 %collective-permute-start.7 = (bf16[8,640]{1,0:T(8,128)(2,1)S(1)}, bf16[8,640]{1,0:T(8,128)(2,1)S(1)}, u32[]{:S(2)}, u32[]{:S(2)}) collective-permute-start(bf16[8,640]{1,0:T(8,128)(2,1)S(1)} %pad_maximum_fusion.11), channel_id=1, source_target_pairs={{0,32},{32,0},{1,33},{33,1},{2,34},{34,2},{3,35},{35,3},{4,36},{36... | collective-permute-start | bytes 30728 | tf_op jit(solution)/shard_map/ppermute | solution.py:160
  148.2 9.5 %copy-start.14 = (bf16[4,640]{1,0:T(4,128)(2,1)S(1)}, bf16[4,640]{1,0:T(4,128)(2,1)}, u32[]{:S(2)}) copy-start(bf16[4,640]{1,0:T(4,128)(2,1)} %copy-done.13) | copy-start | bytes 15364
  148.4 10.6 %copy-start.12 = (bf16[4,640]{1,0:T(4,128)(2,1)S(1)}, bf16[4,640]{1,0:T(4,128)(2,1)}, u32[]{:S(2)}) copy-start(bf16[4,640]{1,0:T(4,128)(2,1)} %copy-done.11) | copy-start | bytes 15364
  148.5 11.8 %collective-permute-start.5 = (bf16[256,768]{1,0:T(8,128)(2,1)S(1)}, bf16[256,768]{1,0:T(8,128)(2,1)S(1)}, u32[]{:S(2)}, u32[]{:S(2)}) collective-permute-start(bf16[256,768]{1,0:T(8,128)(2,1)S(1)} %reshape.174), channel_id=1, source_target_pairs={{0,32},{32,0},{1,33},{33,1},{2,34},{34,2},{3,35},{35,3},{4,36},{36... | collective-permute-start | bytes 1179656 | tf_op jit(solution)/shard_map/ppermute | solution.py:180
  160.3 0.7 copy-start.18
  160.3 0.7 copy-start.20
  161.6 10.3 %copy-start.8 = (bf16[128,256]{1,0:T(8,128)(2,1)S(1)}, bf16[128,256]{1,0:T(8,128)(2,1)}, u32[]{:S(2)}) copy-start(bf16[128,256]{1,0:T(8,128)(2,1)} %copy-done.7) | copy-start | bytes 196612
  161.9 10.9 %copy-start.6 = (bf16[128,256]{1,0:T(8,128)(2,1)S(1)}, bf16[128,256]{1,0:T(8,128)(2,1)}, u32[]{:S(2)}) copy-start(bf16[128,256]{1,0:T(8,128)(2,1)} %copy-done.5) | copy-start | bytes 196612
  161.9 3.2 %collective-permute-start.6 = (f32[4,1280]{1,0:T(4,128)S(1)}, f32[4,1280]{1,0:T(4,128)S(1)}, u32[]{:S(2)}, u32[]{:S(2)}) collective-permute-start(f32[4,1280]{1,0:T(4,128)S(1)} %fusion.77), channel_id=1, source_target_pairs={{0,32},{32,0},{1,33},{33,1},{2,34},{34,2},{3,35},{35,3},{4,36},{36... | collective-permute-start | bytes 61448 | tf_op jit(solution)/shard_map/ppermute | solution.py:198
  165.8 16.1 %all-to-all-start.6 = ((bf16[8,8,640]{2,1,0:T(8,128)(2,1)}), bf16[8,8,640]{2,1,0:T(8,128)(2,1)S(1)}, u32[]{:S(2)}, u32[]{:S(2)}) async-start(bf16[8,8,640]{2,1,0:T(8,128)(2,1)} %broadcast_in_dim.27), calls=%async_computation.6 | async-start | bytes 163840 | tf_op jit(solution)/shard_map/all_to_all | solution.py:45
  (3 other events, 1.9 us)
